TPU v7x, 32 devices: a whole 2x2x4 slice. The times are simulated.
32 devices in a mesh: dp: 4 (over y, x), seq: 8 (over z, core).
Axes of the slice: x: 2, y: 2, z: 4, core: 2. Of those that a mesh axis runs over, the one named last changes fastest.
Arguments:
- hidden_in: bfloat16 [4, 2048, 1024], P('dp', 'seq'), may hold values from -6 to 6
- noise_level: int32 [4, 8], P('dp', 'seq'), may hold values from 0 to 1023
- noise_table: float32 [1024, 1024], P(('dp', 'seq')), may hold values from -6 to 6
- w_ada: float32 [1024, 6144], P(('dp', 'seq')), may hold values from -0.1875 to 0.1875
- b_ada: float32 [6144], P(('dp', 'seq')), may hold values from -3 to 3
- w_qkv: float32 [1024, 3072], P(('dp', 'seq')), may hold values from -0.1875 to 0.1875
- b_qkv: float32 [3072], P(('dp', 'seq')), may hold values from -3 to 3
- w_out: float32 [1024, 1024], P(('dp', 'seq')), may hold values from -0.75 to 0.75
- b_out: float32 [1024], P(('dp', 'seq')), may hold values from -3 to 3
- w_up: float32 [1024, 4096], P(('dp', 'seq')), may hold values from -0.1875 to 0.1875
- b_up: float32 [4096], P(('dp', 'seq')), may hold values from -3 to 3
- w_down: float32 [4096, 1024], P(('dp', 'seq')), may hold values from -0.09375 to 0.09375
- b_down: float32 [1024], P(('dp', 'seq')), may hold values from -3 to 3
- grad_out: bfloat16 [4, 2048, 1024], P('dp', 'seq'), may hold values from -6 to 6
Outputs:
- layer_out: bfloat16 [4, 2048, 1024], P('dp', 'seq')
- grad_hidden: bfloat16 [4, 2048, 1024], P('dp', 'seq')
- grad_noise_table: float32 [1024, 1024], P(('dp', 'seq'))
- grad_w_ada: float32 [1024, 6144], P(('dp', 'seq'))
- grad_b_ada: float32 [6144], P(('dp', 'seq'))
- grad_w_qkv: float32 [1024, 3072], P(('dp', 'seq'))
- grad_b_qkv: float32 [3072], P(('dp', 'seq'))
- grad_w_out: float32 [1024, 1024], P(('dp', 'seq'))
- grad_b_out: float32 [1024], P(('dp', 'seq'))
- grad_w_up: float32 [1024, 4096], P(('dp', 'seq'))
- grad_b_up: float32 [4096], P(('dp', 'seq'))
- grad_w_down: float32 [4096, 1024], P(('dp', 'seq'))
- grad_b_down: float32 [1024], P(('dp', 'seq'))
Inputs may be any that keep to these rules, and one draw needn't show every extreme that they name: `noise_level`: a row of noise_table.
All inputs are finite; a program needn't handle non-finite values.
Results may differ from a plain program's by a relative error of at most 0.038.
Values may be sent and summed in bfloat16 or wider, within the bound.
A program may use at most 192 MiB of HBM per device.

v0:
```python
from functools import partial
import math

import jax
import jax.numpy as jnp
from jax import lax
from jax.sharding import PartitionSpec as P

H = 16
GRID_W = 16
PATCHES = 256


norm_eps = 1e-06
masked_score = -1e30
block_limit = 512


def layer_norm(values):
    centred = values - jnp.mean(values, axis=-1, keepdims=True)
    spread = jnp.mean(centred * centred, axis=-1, keepdims=True)
    return centred * lax.rsqrt(spread + norm_eps)


def modulate(values, shift_term, scale_term):
    return layer_norm(values) * (1.0 + scale_term) + shift_term


def turn_half(values):
    extent = values.shape[-1]
    side_part = 2 * (3 * extent // 16)
    pieces = []
    offset = 0
    for part_size in (extent - 2 * side_part, side_part, side_part):
        half_size = part_size // 2
        pieces.append(-values[..., offset + half_size : offset + part_size])
        pieces.append(values[..., offset : offset + half_size])
        offset = offset + part_size
    return jnp.concatenate(pieces, axis=-1)


def part_angles(places, part_size):
    half_size = part_size // 2
    rates = jnp.exp(-math.log(10000.0) * jnp.arange(half_size, dtype=jnp.float32) / half_size)
    angles = places.astype(jnp.float32)[:, None] * rates[None, :]
    return jnp.concatenate([angles, angles], axis=1)


def angle_table(places, extent):
    side_part = 2 * (3 * extent // 16)
    patch_index = places % PATCHES
    angles = jnp.concatenate(
        [
            part_angles(places // PATCHES, extent - 2 * side_part),
            part_angles(patch_index // GRID_W, side_part),
            part_angles(patch_index % GRID_W, side_part),
        ],
        axis=1,
    )
    return (jnp.cos(angles), jnp.sin(angles))


def rotate(values, cosine_table, sine_table):
    return values * cosine_table + turn_half(values) * sine_table


def unrotate(values, cosine_table, sine_table):
    return values * cosine_table - turn_half(values * sine_table)


def block_split(row_count):
    return row_count // block_limit


def to_blocks(arrived, block_total, head_count, head_dim):
    return arrived.reshape(
        arrived.shape[0], block_total, arrived.shape[1] // block_total, head_count, head_dim
    ).swapaxes(0, 1)


def score_gradients(
    query_block,
    keys_block,
    values_block,
    grad_block,
    total_block,
    delta_block,
    allowed,
    score_scale,
):
    scores = (
        jnp.einsum("cqhd,ckhd->chqk", query_block, keys_block, preferred_element_type=jnp.float32)
        * score_scale
    )
    softmax_weights = jnp.where(allowed, jnp.exp(scores - total_block[..., None]), 0.0)
    grad_soft = jnp.einsum(
        "cqhd,ckhd->chqk", grad_block, values_block, preferred_element_type=jnp.float32
    )
    grad_scores = (softmax_weights * (grad_soft - delta_block[..., None])).astype(jnp.bfloat16)
    query_grad = (
        jnp.einsum("chqk,ckhd->cqhd", grad_scores, keys_block, preferred_element_type=jnp.float32)
        * score_scale
    )
    keys_grad = (
        jnp.einsum("chqk,cqhd->ckhd", grad_scores, query_block, preferred_element_type=jnp.float32)
        * score_scale
    )
    values_grad = jnp.einsum(
        "chqk,cqhd->ckhd",
        softmax_weights.astype(jnp.bfloat16),
        grad_block,
        preferred_element_type=jnp.float32,
    )
    return (query_grad, keys_grad, values_grad)


def body(
    hidden_in,
    noise_level,
    noise_table,
    w_ada,
    b_ada,
    w_qkv,
    b_qkv,
    w_out,
    b_out,
    w_up,
    b_up,
    w_down,
    b_down,
    grad_out,
):
    gathered = (
        lax.all_gather(noise_table.astype(jnp.bfloat16), ("dp", "seq"), axis=0, tiled=True),
        lax.all_gather(w_ada.astype(jnp.bfloat16), ("dp", "seq"), axis=0, tiled=True),
        lax.all_gather(b_ada.astype(jnp.bfloat16), ("dp", "seq"), axis=0, tiled=True),
        lax.all_gather(w_qkv.astype(jnp.bfloat16), ("dp", "seq"), axis=0, tiled=True),
        lax.all_gather(b_qkv.astype(jnp.bfloat16), ("dp", "seq"), axis=0, tiled=True),
        lax.all_gather(w_out.astype(jnp.bfloat16), ("dp", "seq"), axis=0, tiled=True),
        lax.all_gather(b_out.astype(jnp.bfloat16), ("dp", "seq"), axis=0, tiled=True),
        lax.all_gather(w_up.astype(jnp.bfloat16), ("dp", "seq"), axis=0, tiled=True),
        lax.all_gather(b_up.astype(jnp.bfloat16), ("dp", "seq"), axis=0, tiled=True),
        lax.all_gather(w_down.astype(jnp.bfloat16), ("dp", "seq"), axis=0, tiled=True),
        lax.all_gather(b_down.astype(jnp.bfloat16), ("dp", "seq"), axis=0, tiled=True),
    )
    table_low, ada_w, ada_b, qkv_w, qkv_b, out_w, out_b, up_w, up_b, down_w, down_b = gathered
    clip_count, patches, model_width = hidden_in.shape
    head_count = H
    head_dim = model_width // head_count
    score_scale = 1.0 / math.sqrt(head_dim)
    head_shape = (clip_count, patches, head_count, head_dim)
    inputs = hidden_in.astype(jnp.float32)
    one_hot = noise_level[:, 0][:, None] == jnp.arange(table_low.shape[0], dtype=jnp.int32)[None, :]
    embedded = jnp.dot(one_hot.astype(jnp.bfloat16), table_low, preferred_element_type=jnp.float32)
    silu_in = jax.nn.silu(embedded).astype(jnp.bfloat16)
    modulation = jnp.dot(silu_in, ada_w, preferred_element_type=jnp.float32) + ada_b.astype(
        jnp.float32
    )
    shift_one, scale_one, gate_one, shift_two, scale_two, gate_two = [
        modulation[:, None, column_block * model_width : (column_block + 1) * model_width]
        for column_block in range(6)
    ]
    normed_one = modulate(inputs, shift_one, scale_one).astype(jnp.bfloat16)
    qkv_all = jnp.dot(normed_one, qkv_w, preferred_element_type=jnp.float32) + qkv_b.astype(
        jnp.float32
    )
    frame_own = lax.axis_index("seq")
    places = frame_own * patches + jnp.arange(patches, dtype=jnp.int32)
    cosine_local, sine_local = angle_table(places, head_dim)
    cosine_wide = cosine_local[None, :, None, :]
    sine_wide = sine_local[None, :, None, :]
    query_rot = rotate(
        qkv_all[..., :model_width].reshape(head_shape), cosine_wide, sine_wide
    ).astype(jnp.bfloat16)
    keys_rot = rotate(
        qkv_all[..., model_width : 2 * model_width].reshape(head_shape), cosine_wide, sine_wide
    ).astype(jnp.bfloat16)
    values_low = qkv_all[..., 2 * model_width :].astype(jnp.bfloat16)
    query_flat = query_rot.reshape(clip_count, patches, model_width)
    keys_flat = keys_rot.reshape(clip_count, patches, model_width)
    values_heads = values_low.reshape(head_shape)
    initial = (
        jnp.full((clip_count, head_count, patches), masked_score, jnp.float32),
        jnp.zeros((clip_count, head_count, patches), jnp.float32),
        jnp.zeros((clip_count, head_count, patches, head_dim), jnp.float32),
    )
    keys_piece = lax.all_gather(keys_flat, "seq", axis=1, tiled=True)
    values_piece = lax.all_gather(values_low, "seq", axis=1, tiled=True)
    block_total = block_split(keys_piece.shape[1])
    block_rows = keys_piece.shape[1] // block_total

    def one_block(running, block_in):
        row_max, row_total, weighted_sum = running
        keys_block, values_block, block_start = block_in
        allowed = (block_start + jnp.arange(block_rows, dtype=jnp.int32)) // PATCHES <= frame_own
        scores = (
            jnp.einsum("cqhd,ckhd->chqk", query_rot, keys_block, preferred_element_type=jnp.float32)
            * score_scale
        )
        scores = jnp.where(allowed, scores, masked_score)
        new_max = jnp.maximum(row_max, jnp.max(scores, axis=-1))
        kept_share = jnp.exp(row_max - new_max)
        exponent = jnp.where(allowed, jnp.exp(scores - new_max[..., None]), 0.0)
        row_total = row_total * kept_share + jnp.sum(exponent, axis=-1)
        weighted_sum = weighted_sum * kept_share[..., None] + jnp.einsum(
            "chqk,ckhd->chqd",
            exponent.astype(jnp.bfloat16),
            values_block,
            preferred_element_type=jnp.float32,
        )
        return ((new_max, row_total, weighted_sum), None)

    starts = jnp.arange(block_total, dtype=jnp.int32) * block_rows
    result, unused = lax.scan(
        one_block,
        initial,
        (
            to_blocks(keys_piece, block_total, head_count, head_dim),
            to_blocks(values_piece, block_total, head_count, head_dim),
            starts,
        ),
    )
    row_max, row_total, weighted_sum = result
    log_total = row_max + jnp.log(row_total)
    attended = (
        (weighted_sum / row_total[..., None])
        .transpose(0, 2, 1, 3)
        .reshape(clip_count, patches, model_width)
    )
    attended_low = attended.astype(jnp.bfloat16)
    branch_one = jnp.dot(attended_low, out_w, preferred_element_type=jnp.float32) + out_b.astype(
        jnp.float32
    )
    middle = inputs + gate_one * branch_one
    normed_two = modulate(middle, shift_two, scale_two).astype(jnp.bfloat16)
    hidden_pre = jnp.dot(normed_two, up_w, preferred_element_type=jnp.float32) + up_b.astype(
        jnp.float32
    )
    hidden_act = jax.nn.gelu(hidden_pre, approximate=True).astype(jnp.bfloat16)
    branch_two = jnp.dot(hidden_act, down_w, preferred_element_type=jnp.float32) + down_b.astype(
        jnp.float32
    )
    outputs = middle + gate_two * branch_two
    back_weights = (
        lax.all_gather(w_ada.astype(jnp.bfloat16), ("dp", "seq"), axis=0, tiled=True),
        lax.all_gather(w_qkv.astype(jnp.bfloat16), ("dp", "seq"), axis=0, tiled=True),
        lax.all_gather(w_out.astype(jnp.bfloat16), ("dp", "seq"), axis=0, tiled=True),
        lax.all_gather(w_up.astype(jnp.bfloat16), ("dp", "seq"), axis=0, tiled=True),
        lax.all_gather(w_down.astype(jnp.bfloat16), ("dp", "seq"), axis=0, tiled=True),
    )
    ada_back, qkv_back, out_back, up_back, down_back = back_weights
    cotangent = grad_out.astype(jnp.float32)
    grad_gate_two = jnp.sum(cotangent * branch_two, axis=1)
    grad_branch_two = (cotangent * gate_two).astype(jnp.bfloat16)
    grad_down_w = jnp.einsum(
        "cpf,cpd->fd", hidden_act, grad_branch_two, preferred_element_type=jnp.float32
    )
    grad_down_b = jnp.sum(grad_branch_two.astype(jnp.float32), axis=(0, 1))
    grad_act = jnp.einsum(
        "cpd,fd->cpf", grad_branch_two, down_back, preferred_element_type=jnp.float32
    )
    unused, gelu_back = jax.vjp(partial(jax.nn.gelu, approximate=True), hidden_pre)
    grad_pre = gelu_back(grad_act)[0].astype(jnp.bfloat16)
    grad_up_w = jnp.einsum("cpd,cpf->df", normed_two, grad_pre, preferred_element_type=jnp.float32)
    grad_up_b = jnp.sum(grad_pre.astype(jnp.float32), axis=(0, 1))
    grad_normed_two = jnp.einsum(
        "cpf,df->cpd", grad_pre, up_back, preferred_element_type=jnp.float32
    )
    unused, norm_two_back = jax.vjp(modulate, middle, shift_two, scale_two)
    grad_middle_norm, grad_shift_two, grad_scale_two = norm_two_back(grad_normed_two)
    grad_middle = cotangent + grad_middle_norm
    grad_gate_one = jnp.sum(grad_middle * branch_one, axis=1)
    grad_branch_one = (grad_middle * gate_one).astype(jnp.bfloat16)
    grad_out_w = jnp.einsum(
        "cpi,cpo->io", attended_low, grad_branch_one, preferred_element_type=jnp.float32
    )
    grad_out_b = jnp.sum(grad_branch_one.astype(jnp.float32), axis=(0, 1))
    grad_attended = jnp.einsum(
        "cpo,io->cpi", grad_branch_one, out_back, preferred_element_type=jnp.float32
    ).astype(jnp.bfloat16)
    grad_heads = grad_attended.reshape(head_shape)
    row_delta = jnp.sum(
        grad_heads.astype(jnp.float32) * attended_low.astype(jnp.float32).reshape(head_shape),
        axis=-1,
    ).transpose(0, 2, 1)
    keys_piece = lax.all_gather(keys_flat, "seq", axis=1, tiled=True)
    values_piece = lax.all_gather(values_low, "seq", axis=1, tiled=True)
    block_total = block_split(keys_piece.shape[1])
    fold_block_rows = keys_piece.shape[1] // block_total

    def one_block(running, block_in):
        keys_block, values_block, block_start = block_in
        allowed = (
            block_start + jnp.arange(fold_block_rows, dtype=jnp.int32)
        ) // PATCHES <= frame_own
        query_grad, unused_keys, unused_values = score_gradients(
            query_rot,
            keys_block,
            values_block,
            grad_heads,
            log_total,
            row_delta,
            allowed,
            score_scale,
        )
        return (running + query_grad, None)

    starts = jnp.arange(block_total, dtype=jnp.int32) * fold_block_rows
    result, unused = lax.scan(
        one_block,
        jnp.zeros(head_shape, jnp.float32),
        (
            to_blocks(keys_piece, block_total, head_count, head_dim),
            to_blocks(values_piece, block_total, head_count, head_dim),
            starts,
        ),
    )
    grad_query = result

    def fold_keys(carried, arrived):
        query_piece, grad_piece, total_piece, delta_piece = arrived
        row_count = query_piece.shape[1]
        block_total = block_split(row_count)
        block_rows = row_count // block_total
        query_blocks = to_blocks(
            query_piece.astype(jnp.bfloat16), block_total, head_count, head_dim
        )
        grad_blocks = to_blocks(grad_piece.astype(jnp.bfloat16), block_total, head_count, head_dim)
        total_blocks = total_piece.reshape(
            clip_count, block_total, block_rows, head_count
        ).transpose(1, 0, 3, 2)
        delta_blocks = delta_piece.reshape(
            clip_count, block_total, block_rows, head_count
        ).transpose(1, 0, 3, 2)

        def one_block(running, block_in):
            query_block, grad_block, total_block, delta_block, block_start = block_in
            allowed = (
                (block_start + jnp.arange(block_rows, dtype=jnp.int32)) // PATCHES >= frame_own
            )[:, None]
            unused_query, keys_grad, values_grad = score_gradients(
                query_block,
                keys_rot,
                values_heads,
                grad_block,
                total_block,
                delta_block,
                allowed,
                score_scale,
            )
            return ((running[0] + keys_grad, running[1] + values_grad), None)

        starts = jnp.arange(block_total, dtype=jnp.int32) * block_rows
        result, unused = lax.scan(
            one_block, carried, (query_blocks, grad_blocks, total_blocks, delta_blocks, starts)
        )
        return result

    initial = (jnp.zeros(head_shape, jnp.float32), jnp.zeros(head_shape, jnp.float32))
    grad_keys, grad_values = fold_keys(
        initial,
        (
            lax.all_gather(query_flat.astype(jnp.float32), "seq", axis=1, tiled=True),
            lax.all_gather(grad_attended.astype(jnp.float32), "seq", axis=1, tiled=True),
            lax.all_gather(log_total.transpose(0, 2, 1), "seq", axis=1, tiled=True),
            lax.all_gather(row_delta.transpose(0, 2, 1), "seq", axis=1, tiled=True),
        ),
    )
    grad_q_pre = (
        unrotate(grad_query, cosine_wide, sine_wide)
        .reshape(clip_count, patches, model_width)
        .astype(jnp.bfloat16)
    )
    grad_k_pre = (
        unrotate(grad_keys, cosine_wide, sine_wide)
        .reshape(clip_count, patches, model_width)
        .astype(jnp.bfloat16)
    )
    grad_v_pre = grad_values.reshape(clip_count, patches, model_width).astype(jnp.bfloat16)
    grad_qkv = jnp.concatenate([grad_q_pre, grad_k_pre, grad_v_pre], axis=-1)
    grad_qkv_w = jnp.einsum("cpd,cpe->de", normed_one, grad_qkv, preferred_element_type=jnp.float32)
    grad_qkv_b = jnp.sum(grad_qkv.astype(jnp.float32), axis=(0, 1))
    grad_normed_one = jnp.einsum(
        "cpe,de->cpd", grad_qkv, qkv_back, preferred_element_type=jnp.float32
    )
    unused, norm_one_back = jax.vjp(modulate, inputs, shift_one, scale_one)
    grad_input_norm, grad_shift_one, grad_scale_one = norm_one_back(grad_normed_one)
    grad_input = grad_middle + grad_input_norm
    grad_modulation = jnp.concatenate(
        [
            grad_shift_one[:, 0],
            grad_scale_one[:, 0],
            grad_gate_one,
            grad_shift_two[:, 0],
            grad_scale_two[:, 0],
            grad_gate_two,
        ],
        axis=-1,
    ).astype(jnp.bfloat16)
    grad_ada_w = jnp.dot(silu_in.T, grad_modulation, preferred_element_type=jnp.float32)
    grad_ada_b = jnp.sum(grad_modulation.astype(jnp.float32), axis=0)
    grad_silu = jnp.einsum(
        "ce,de->cd", grad_modulation, ada_back, preferred_element_type=jnp.float32
    )
    unused, silu_back = jax.vjp(jax.nn.silu, embedded)
    grad_embedded = silu_back(grad_silu)[0]
    grad_table = jnp.dot(
        one_hot.astype(jnp.float32).T, grad_embedded, precision=lax.Precision.HIGHEST
    )
    shares = (
        lax.psum_scatter(grad_table, ("dp", "seq"), scatter_dimension=0, tiled=True),
        lax.psum_scatter(grad_ada_w, ("dp", "seq"), scatter_dimension=0, tiled=True),
        lax.psum_scatter(grad_ada_b, ("dp", "seq"), scatter_dimension=0, tiled=True),
        lax.psum_scatter(grad_qkv_w, ("dp", "seq"), scatter_dimension=0, tiled=True),
        lax.psum_scatter(grad_qkv_b, ("dp", "seq"), scatter_dimension=0, tiled=True),
        lax.psum_scatter(grad_out_w, ("dp", "seq"), scatter_dimension=0, tiled=True),
        lax.psum_scatter(grad_out_b, ("dp", "seq"), scatter_dimension=0, tiled=True),
        lax.psum_scatter(grad_up_w, ("dp", "seq"), scatter_dimension=0, tiled=True),
        lax.psum_scatter(grad_up_b, ("dp", "seq"), scatter_dimension=0, tiled=True),
        lax.psum_scatter(grad_down_w, ("dp", "seq"), scatter_dimension=0, tiled=True),
        lax.psum_scatter(grad_down_b, ("dp", "seq"), scatter_dimension=0, tiled=True),
    )
    return (
        outputs.astype(jnp.bfloat16),
        grad_input.astype(jnp.bfloat16),
        shares[0],
        shares[1],
        shares[2],
        shares[3],
        shares[4],
        shares[5],
        shares[6],
        shares[7],
        shares[8],
        shares[9],
        shares[10],
    )


def solution(mesh):
    placed = (
        P("dp", "seq", None),
        P("dp", "seq"),
        P(("dp", "seq"), None),
        P(("dp", "seq"), None),
        P(("dp", "seq")),
        P(("dp", "seq"), None),
        P(("dp", "seq")),
        P(("dp", "seq"), None),
        P(("dp", "seq")),
        P(("dp", "seq"), None),
        P(("dp", "seq")),
        P(("dp", "seq"), None),
        P(("dp", "seq")),
        P("dp", "seq", None),
    )
    return jax.shard_map(
        body,
        mesh=mesh,
        in_specs=placed,
        out_specs=(
            P("dp", "seq", None),
            P("dp", "seq", None),
            P(("dp", "seq"), None),
            P(("dp", "seq"), None),
            P(("dp", "seq")),
            P(("dp", "seq"), None),
            P(("dp", "seq")),
            P(("dp", "seq"), None),
            P(("dp", "seq")),
            P(("dp", "seq"), None),
            P(("dp", "seq")),
            P(("dp", "seq"), None),
            P(("dp", "seq")),
        ),
        check_vma=False,
    )
```

profile of v0, /device:TPU:0, one launch (start us, length us, event | category | flops | bytes accessed | tf_op | source)
XLA Modules:
  0.0 1848.2 jit_solution(778534063473432318)
XLA Ops:
  16.8 42.5 %all-reduce.10 = (bf16[3072]{0:T(1024)(128)(2,1)S(1)}, bf16[6144]{0:T(1024)(128)(2,1)S(1)}, bf16[1024]{0:T(1024)(128)(2,1)S(1)}, bf16[1024]{0:T(1024)(128)(2,1)S(1)}) all-reduce(bf16[3072]{0:T(1024)(128)(2,1)S(1)} %dynamic-update-slice.1, bf16[6144]{0:T(1024)(128)(2,1)S(1)} %dynamic-update-slice, ...), channel_id=1, replica_groups=mesh['dp'=4,'seq'=8] {'dp','seq'}, use_global_device_ids=true, to_apply=%add.1 | all-reduce | flops 11264 | bytes 45056
  73.5 96.0 %all-gather.16.cloned.1.call-done = bf16[1024,6144]{1,0:T(8,128)(2,1)} async-done(((bf16[32,6144]{1,0:T(8,128)(2,1)}), bf16[1024,6144]{1,0:T(8,128)(2,1)}) %all-gather.16.cloned.1.call-update) | async-done | bytes 12582928 | tf_op jit(solution)/shard_map/all_gather | solution.py:135
  175.9 65.0 %all-gather.18.cloned.1.call-done = bf16[1024,3072]{1,0:T(8,128)(2,1)} async-done(((bf16[32,3072]{1,0:T(8,128)(2,1)}), bf16[1024,3072]{1,0:T(8,128)(2,1)}) %all-gather.18.cloned.1.call-update) | async-done | bytes 6291472 | tf_op jit(solution)/shard_map/all_gather | solution.py:137
  289.0 39.6 %all-gather.2 = bf16[32,1,128]{2,1,0:T(2,128)(2,1)S(1)} all-gather(bf16[1,1,128]{2,1,0:T(2,128)(2,1)S(1)} %convert_bitcast_fusion), channel_id=1, replica_groups=mesh['dp'=4,'seq'=8] {'dp','seq'}, dimensions={0}, use_global_device_ids=true | all-gather | bytes 8448 | tf_op jit(solution)/shard_map/all_gather | solution.py:142
  331.8 11.6 reshape.1207
  353.2 24.0 %all-gather.22.cloned.1.call-done = bf16[1,2048,1024]{2,1,0:T(8,128)(2,1)} async-done(((bf16[1,256,1024]{2,1,0:T(8,128)(2,1)}), bf16[1,2048,1024]{2,1,0:T(8,128)(2,1)}) %all-gather.22.cloned.1.call-update) | async-done | bytes 4194320 | tf_op jit(solution)/shard_map/all_gather | solution.py:188
  398.7 68.8 %while.45 = (s32[]{:T(128)}, f32[1,16,256]{2,1,0:T(8,128)S(1)}, f32[1,16,256]{2,1,0:T(8,128)S(1)}, f32[1,16,256,64]{2,3,1,0:T(8,128)S(1)}, s32[4]{0:T(128)S(1)},...) while((s32[]{:T(128)}, f32[1,16,256]{2,1,0:T(8,128)S(1)}, ...), condition=%wide.region_5.6_spmd.clone, body=%wide.region_2.5_spmd.clone.sunk | while | flops 564953600 | bytes 63703736 | solution.py:214
  472.0 43.6 %all-gather.26.cloned.1.call-done = bf16[1024,4096]{1,0:T(8,128)(2,1)} async-done(((bf16[32,4096]{1,0:T(8,128)(2,1)}), bf16[1024,4096]{1,0:T(8,128)(2,1)}) %all-gather.26.cloned.1.call-update) | async-done | bytes 8388624 | tf_op jit(solution)/shard_map/all_gather | solution.py:141
  523.5 71.7 %all-gather.28.cloned.1.call-done = bf16[4096,1024]{1,0:T(8,128)(2,1)} async-done(((bf16[128,1024]{1,0:T(8,128)(2,1)}), bf16[4096,1024]{1,0:T(8,128)(2,1)}) %all-gather.28.cloned.1.call-update) | async-done | bytes 8388624 | tf_op jit(solution)/shard_map/all_gather | solution.py:143
  595.2 12.3 convert_reduce_fusion
  625.4 17.8 all-gather.30.cloned.1.call-done
  643.1 11.7 reshape.1205
  664.7 14.4 all_gather.72
  680.5 15.4 all-gather.1
  701.1 62.6 %while.46 = (s32[]{:T(128)}, f32[1,256,16,64]{1,3,2,0:T(8,128)}, bf16[4,1,512,16,64]{2,4,3,1,0:T(8,128)(2,1)}, s32[4]{0:T(128)S(1)}, s32[]{:T(128)}, /*index=5*/...) while((s32[]{:T(128)}, f32[1,256,16,64]{1,3,2,0:T(8,128)}, ...), condition=%wide.region_12.13_spmd.clone, body=%wide.region_11.12_spmd.clone.sunk | while | flops 818684416 | bytes 31492820 | solution.py:309
  785.5 83.9 %while.47 = (s32[]{:T(128)}, f32[1,256,16,64]{1,3,2,0:T(8,128)S(1)}, f32[1,256,16,64]{1,3,2,0:T(8,128)}, bf16[4,1,512,16,64]{2,4,3,1,0:T(8,128)(2,1)}, s32[4]{0:...) while((s32[]{:T(128)}, ...), condition=%wide.region_14.15_spmd.clone, body=%wide.region_13.14_spmd.clone.sunk | while | flops 1096032768 | bytes 34966700 | solution.py:354
  882.6 11.7 concatenate.70
  944.0 11.6 broadcast_multiply_fusion
  957.3 39.5 %all-reduce.9 = (f32[6144]{0:T(1024)S(1)}, f32[3072]{0:T(1024)S(1)}, f32[1024]{0:T(1024)S(1)}, f32[4096]{0:T(1024)S(1)}, f32[1024]{0:T(1024)S(1)}) all-reduce(bf16[6144]{0:T(1024)(128)(2,1)S(1)} %constant_dynamic-update-slice_fusion, f32[3072]{0:T(1024)S(1)} %convert_reduce_fusion.1, ...), channel_id=6, replica_groups=mesh['dp'=4,'seq'=8] {'dp','seq'}, use_global_device_ids=true, to_apply=%region_25.26.clone | all-reduce | flops 15360 | bytes 110592
  1002.4 52.4 %reduce-scatter.7.cloned.1.call-done = f32[32,1024]{1,0:T(8,128)} async-done(((f32[1024,1024]{1,0:T(8,128)}), f32[32,1024]{1,0:T(8,128)}) %reduce-scatter.7.cloned.1.call-update) | async-done | bytes 131088 | tf_op jit(solution)/shard_map/reduce_scatter | solution.py:411
  1054.8 159.4 %reduce-scatter.11.cloned.1.call-done = f32[32,3072]{1,0:T(8,128)} async-done(((f32[1024,3072]{1,0:T(8,128)}), f32[32,3072]{1,0:T(8,128)}) %reduce-scatter.11.cloned.1.call-update) | async-done | bytes 393232 | tf_op jit(solution)/shard_map/reduce_scatter | solution.py:414
  1214.2 188.6 %reduce-scatter.15.cloned.1.call-done = f32[32,4096]{1,0:T(8,128)} async-done(((f32[1024,4096]{1,0:T(8,128)}), f32[32,4096]{1,0:T(8,128)}) %reduce-scatter.15.cloned.1.call-update) | async-done | bytes 524304 | tf_op jit(solution)/shard_map/reduce_scatter | solution.py:418
  1402.8 187.2 %reduce-scatter.17.cloned.1.call-done = f32[128,1024]{1,0:T(8,128)} async-done(((f32[4096,1024]{1,0:T(8,128)}), f32[128,1024]{1,0:T(8,128)}) %reduce-scatter.17.cloned.1.call-update) | async-done | bytes 524304 | tf_op jit(solution)/shard_map/reduce_scatter | solution.py:420
  1590.0 251.2 %reduce-scatter.9.cloned.1.call-done = f32[32,6144]{1,0:T(8,128)} async-done(((f32[1024,6144]{1,0:T(8,128)}), f32[32,6144]{1,0:T(8,128)}) %reduce-scatter.9.cloned.1.call-update) | async-done | bytes 786448 | tf_op jit(solution)/shard_map/reduce_scatter | solution.py:412
  (387 shorter events, 464.6 us)
Async XLA Ops:
  7.2 63.7 %all-gather.14.cloned.1.call-start = ((), (), s32[]{:S(2)}) async-start(), calls=%async_computation.6 | async-start | bytes 2162688 | tf_op jit(solution)/shard_map/all_gather | solution.py:134
  8.8 160.7 %all-gather.16.cloned.1.call-start = ((), (), s32[]{:S(2)}) async-start(), calls=%async_computation.7 | async-start | bytes 12976128 | tf_op jit(solution)/shard_map/all_gather | solution.py:135
  10.8 230.0 %all-gather.18.cloned.1.call-start = ((), (), s32[]{:S(2)}) async-start(), calls=%async_computation.8 | async-start | bytes 6488064 | tf_op jit(solution)/shard_map/all_gather | solution.py:137
  12.6 319.2 %all-gather.20.cloned.1.call-start = ((), (), s32[]{:S(2)}) async-start(), calls=%async_computation.9 | async-start | bytes 4718592 | tf_op jit(solution)/shard_map/all_gather | solution.py:187
  60.0 268.6 %copy-start.24 = (f32[256,64]{0,1:T(8,128)}, f32[256,64]{0,1:T(8,128)S(1)}, u32[]{:S(2)}) copy-start(f32[256,64]{0,1:T(8,128)S(1)} %get-tuple-element.717) | copy-start | bytes 196612
  60.0 268.6 %copy-start.26 = (f32[256,64]{0,1:T(8,128)}, f32[256,64]{0,1:T(8,128)S(1)}, u32[]{:S(2)}) copy-start(f32[256,64]{0,1:T(8,128)S(1)} %get-tuple-element.716) | copy-start | bytes 196612
  63.0 177.8 %copy-start.43 = (f32[256]{0:T(256)}, f32[256]{0:T(256)S(1)}, u32[]{:S(2)}) copy-start(f32[256]{0:T(256)S(1)} %broadcast_multiply_fusion.8) | copy-start | bytes 3076
  63.9 176.9 %copy-start.41 = (f32[256]{0:T(256)}, f32[256]{0:T(256)S(1)}, u32[]{:S(2)}) copy-start(f32[256]{0:T(256)S(1)} %fusion.150) | copy-start | bytes 3076
  175.8 339.8 %copy-start.34 = (f32[1,1024]{1,0:T(1,128)}, f32[1,1024]{1,0:T(1,128)S(1)}, u32[]{:S(2)}) copy-start(f32[1,1024]{1,0:T(1,128)S(1)} %get-tuple-element.719) | copy-start | bytes 12292
  175.9 438.5 %copy-start.30 = (f32[1,1024]{1,0:T(1,128)}, f32[1,1024]{1,0:T(1,128)S(1)}, u32[]{:S(2)}) copy-start(f32[1,1024]{1,0:T(1,128)S(1)} %get-tuple-element.720) | copy-start | bytes 12292
  175.9 439.0 %copy-start.49 = (f32[1,1024]{1,0:T(1,128)}, f32[1,1024]{1,0:T(1,128)S(1)}, u32[]{:S(2)}) copy-start(f32[1,1024]{1,0:T(1,128)S(1)} %get-tuple-element.718) | copy-start | bytes 12292
  283.4 93.9 %all-gather.22.cloned.1.call-start = ((), (), s32[]{:S(2)}) async-start(), calls=%async_computation.10 | async-start | bytes 4718592 | tf_op jit(solution)/shard_map/all_gather | solution.py:188
  285.5 182.1 %all-gather.24.cloned.1.call-start = ((), (), s32[]{:S(2)}) async-start(), calls=%async_computation.11 | async-start | bytes 2162688 | tf_op jit(solution)/shard_map/all_gather | solution.py:139
  286.2 229.4 %all-gather.26.cloned.1.call-start = ((), (), s32[]{:S(2)}) async-start(), calls=%async_computation.12 | async-start | bytes 8650752 | tf_op jit(solution)/shard_map/all_gather | solution.py:141
  287.1 308.1 %all-gather.28.cloned.1.call-start = ((), (), s32[]{:S(2)}) async-start(), calls=%async_computation.13 | async-start | bytes 8650752 | tf_op jit(solution)/shard_map/all_gather | solution.py:143
  288.9 354.2 %all-gather.30.cloned.1.call-start = ((), (), s32[]{:S(2)}) async-start(), calls=%async_computation.14 | async-start | bytes 4718592 | tf_op jit(solution)/shard_map/all_gather | solution.py:363
  331.5 432.5 %all-gather.32.cloned.1.call-start = ((), (), s32[]{:S(2)}) async-start(), calls=%async_computation.21 | async-start | bytes 4718592 | tf_op jit(solution)/shard_map/all_gather | solution.py:364
  471.8 142.6 %copy-start.45 = (f32[256]{0:T(256)}, f32[256]{0:T(256)S(1)}, u32[]{:S(2)}) copy-start(f32[256]{0:T(256)S(1)} %broadcast_multiply_fusion.7) | copy-start | bytes 3076
  623.0 379.4 %reduce-scatter.13.cloned.1.call-start = ((), (), s32[]{:S(2)}) async-start(), calls=%async_computation.18 | async-start | bytes 4325376 | tf_op jit(solution)/shard_map/reduce_scatter | solution.py:416
  763.7 291.1 %reduce-scatter.7.cloned.1.call-start = ((), (), s32[]{:S(2)}) async-start(), calls=%async_computation.15 | async-start | bytes 4325376 | tf_op jit(solution)/shard_map/reduce_scatter | solution.py:411
  913.0 301.2 %reduce-scatter.11.cloned.1.call-start = ((), (), s32[]{:S(2)}) async-start(), calls=%async_computation.17 | async-start | bytes 12976128 | tf_op jit(solution)/shard_map/reduce_scatter | solution.py:414
  920.9 481.9 %reduce-scatter.15.cloned.1.call-start = ((), (), s32[]{:S(2)}) async-start(), calls=%async_computation.19 | async-start | bytes 17301504 | tf_op jit(solution)/shard_map/reduce_scatter | solution.py:418
  931.4 658.6 %reduce-scatter.17.cloned.1.call-start = ((), (), s32[]{:S(2)}) async-start(), calls=%async_computation.20 | async-start | bytes 17301504 | tf_op jit(solution)/shard_map/reduce_scatter | solution.py:420
  943.3 897.8 %reduce-scatter.9.cloned.1.call-start = ((), (), s32[]{:S(2)}) async-start(), calls=%async_computation.16 | async-start | bytes 25952256 | tf_op jit(solution)/shard_map/reduce_scatter | solution.py:412
  (62 other events, 943.7 us)
Sparse Core Ops, SparseCore 0:
  11.6 59.2 all-gather.13
  74.4 94.9 all-gather.15
  173.1 67.7 all-gather.17
  283.5 45.7 all-gather.19
  331.3 45.8 all-gather.21
  380.6 55.1 all-gather.23
  439.4 76.1 all-gather.25
  519.2 75.9 all-gather.27
  597.4 45.7 all-gather.29
  645.2 47.6 all-gather.31
  763.8 141.8 reduce-scatter.12
  913.1 141.6 reduce-scatter.6
  1061.4 152.7 reduce-scatter.10
  1217.0 185.7 reduce-scatter.14
  1405.6 184.3 reduce-scatter.16
  1598.0 243.1 reduce-scatter.8
where the time goes:
time: 1860 us; the launch traced here: 1850 us
  waiting for transfers between devices  1160 us (62%)
  matrix products  266 us (14%)
  local copies, waits for them, and re-layouts  168 us (9%)
  blocking collectives  151 us (8%)
  other arithmetic  80.5 us (4%)
    reduce_scatter x1, waiting for transfers between devices, body(): lax.psum_scatter(grad_ada_w, ('dp', 'seq'), scatter_dimension=0, tiled=True)  251 us
    reduce_scatter x1, waiting for transfers between devices, body(): lax.psum_scatter(grad_up_w, ('dp', 'seq'), scatter_dimension=0, tiled=True)  189 us
    reduce_scatter x1, waiting for transfers between devices, body(): lax.psum_scatter(grad_down_w, ('dp', 'seq'), scatter_dimension=0, tiled=T...  187 us
    reduce_scatter x1, waiting for transfers between devices, body(): lax.psum_scatter(grad_qkv_w, ('dp', 'seq'), scatter_dimension=0, tiled=True)  159 us
    all_gather x1, waiting for transfers between devices, body(): lax.all_gather(w_ada.astype(jnp.bfloat16), ('dp', 'seq'), axis=0, tiled=T...  96 us
    unnamed x2, blocking collectives  82 us
    all_gather x1, waiting for transfers between devices, body(): lax.all_gather(w_down.astype(jnp.bfloat16), ('dp', 'seq'), axis=0, tiled=...  71.7 us
    all_gather x1, waiting for transfers between devices, body(): lax.all_gather(w_qkv.astype(jnp.bfloat16), ('dp', 'seq'), axis=0, tiled=T...  65 us
  transfers between devices with their start and end apart: 16, of which 12 were waited for; matrix products, arithmetic and copies ran while one was open for 25% of the time, Pallas kernels for 0%

commit v1 on v0

v1 whole, which is shorter than its diff:
```python
from functools import partial
import math

import jax
import jax.numpy as jnp
from jax import lax
from jax.sharding import PartitionSpec as P

H = 16
GRID_W = 16
PATCHES = 256


norm_eps = 1e-06
masked_score = -1e30
ALL = ("dp", "seq")
F32 = jnp.float32
BF16 = jnp.bfloat16


def layer_norm(values):
    centred = values - jnp.mean(values, axis=-1, keepdims=True)
    spread = jnp.mean(centred * centred, axis=-1, keepdims=True)
    return centred * lax.rsqrt(spread + norm_eps)


def modulate(values, shift_term, scale_term):
    return layer_norm(values) * (1.0 + scale_term) + shift_term


def turn_half(values):
    extent = values.shape[-1]
    side_part = 2 * (3 * extent // 16)
    pieces = []
    offset = 0
    for part_size in (extent - 2 * side_part, side_part, side_part):
        half_size = part_size // 2
        pieces.append(-values[..., offset + half_size : offset + part_size])
        pieces.append(values[..., offset : offset + half_size])
        offset = offset + part_size
    return jnp.concatenate(pieces, axis=-1)


def part_angles(places, part_size):
    half_size = part_size // 2
    rates = jnp.exp(-math.log(10000.0) * jnp.arange(half_size, dtype=F32) / half_size)
    angles = places.astype(F32)[:, None] * rates[None, :]
    return jnp.concatenate([angles, angles], axis=1)


def angle_table(places, extent):
    side_part = 2 * (3 * extent // 16)
    patch_index = places % PATCHES
    angles = jnp.concatenate(
        [
            part_angles(places // PATCHES, extent - 2 * side_part),
            part_angles(patch_index // GRID_W, side_part),
            part_angles(patch_index % GRID_W, side_part),
        ],
        axis=1,
    )
    return (jnp.cos(angles), jnp.sin(angles))


def rotate(values, cosine_table, sine_table):
    return values * cosine_table + turn_half(values) * sine_table


def unrotate(values, cosine_table, sine_table):
    return values * cosine_table - turn_half(values * sine_table)


def low(values):
    return values.astype(BF16)


def dot(left, right):
    return jnp.dot(left, right, preferred_element_type=F32)


def gather_rows(share):
    return lax.all_gather(low(share), ALL, axis=0, tiled=True)


def scatter_rows(whole):
    return lax.psum_scatter(whole, ALL, scatter_dimension=0, tiled=True)


def frame_modulation(noise_level, noise_table, w_ada, b_ada):
    levels = lax.all_gather(noise_level.reshape(-1), ALL, axis=0, tiled=True)
    device = lax.axis_index("dp") * lax.axis_size("seq") + lax.axis_index("seq")
    share = noise_table.shape[0]
    own_levels = device * share + jnp.arange(share, dtype=jnp.int32)
    one_hot = levels[:, None] == own_levels[None, :]
    found = dot(low(one_hot), low(noise_table))
    embedded = lax.psum_scatter(low(found), ALL, scatter_dimension=1, tiled=True).astype(F32)
    silu_in = low(jax.nn.silu(embedded))
    modulation = lax.psum_scatter(
        dot(silu_in, low(w_ada)), ALL, scatter_dimension=0, tiled=True
    ) + gather_rows(b_ada).astype(F32)
    return one_hot, embedded, silu_in, modulation


def frame_gradients(grad_modulation, one_hot, embedded, silu_in, w_ada):
    every = lax.all_gather(grad_modulation, ALL, axis=0, tiled=True)
    grad_ada_w = lax.dot_general(
        silu_in, every, (((0,), (0,)), ((), ())), preferred_element_type=F32
    )
    share = w_ada.shape[1] // lax.axis_size(ALL)
    device = lax.axis_index("dp") * lax.axis_size("seq") + lax.axis_index("seq")
    columns = lax.dynamic_slice_in_dim(every, device * share, share, axis=1)
    grad_ada_b = jnp.sum(columns.astype(F32), axis=0)
    grad_silu = lax.dot_general(
        every, low(w_ada), (((1,), (1,)), ((), ())), preferred_element_type=F32
    )
    unused, silu_back = jax.vjp(jax.nn.silu, embedded)
    grad_embedded = lax.all_gather(silu_back(grad_silu)[0], ALL, axis=1, tiled=True)
    grad_table = jnp.dot(
        one_hot.astype(F32).T, grad_embedded, precision=lax.Precision.HIGHEST
    )
    return grad_table, grad_ada_w, grad_ada_b


def to_heads(values):
    return lax.all_to_all(values, "seq", split_axis=2, concat_axis=1, tiled=True)


def to_tokens(values):
    return lax.all_to_all(values, "seq", split_axis=1, concat_axis=2, tiled=True)


def as_heads(values):
    return values.reshape(*values.shape[:2], -1, 64)


def query_blocks(array, axis):
    blocks = array.shape[axis] // PATCHES
    split = array.shape[:axis] + (blocks, PATCHES) + array.shape[axis + 1 :]
    return jnp.moveaxis(array.reshape(split), axis, 0)


def block_scores(query_block, keys, frame, score_scale):
    scores = (
        jnp.einsum("cqhd,ckhd->chqk", query_block, keys, preferred_element_type=F32) * score_scale
    )
    allowed = jnp.arange(keys.shape[1], dtype=jnp.int32) // PATCHES <= frame
    return jnp.where(allowed, scores, masked_score)


def attend(query, keys, values, score_scale):
    def one_block(block_in):
        query_block, frame = block_in
        scores = block_scores(query_block, keys, frame, score_scale)
        row_max = jnp.max(scores, axis=-1, keepdims=True)
        exponent = jnp.exp(scores - row_max)
        row_total = jnp.sum(exponent, axis=-1, keepdims=True)
        weighted = jnp.einsum(
            "chqk,ckhd->cqhd", low(exponent / row_total), values, preferred_element_type=F32
        )
        return low(weighted), (row_max + jnp.log(row_total))[..., 0]

    frames = jnp.arange(query.shape[1] // PATCHES, dtype=jnp.int32)
    attended, log_total = lax.map(one_block, (query_blocks(query, 1), frames))
    return (
        jnp.moveaxis(attended, 0, 1).reshape(query.shape),
        jnp.moveaxis(log_total, 0, 2).reshape(query.shape[0], query.shape[2], query.shape[1]),
    )


def attend_back(query, keys, values, grad_heads, log_total, row_delta, score_scale):
    def one_block(carried, block_in):
        query_block, grad_block, total_block, delta_block, frame = block_in
        scores = block_scores(query_block, keys, frame, score_scale)
        softmax_weights = jnp.exp(scores - total_block[..., None])
        grad_soft = jnp.einsum("cqhd,ckhd->chqk", grad_block, values, preferred_element_type=F32)
        grad_scores = low(softmax_weights * (grad_soft - delta_block[..., None]))
        query_grad = jnp.einsum("chqk,ckhd->cqhd", grad_scores, keys, preferred_element_type=F32)
        keys_grad = jnp.einsum(
            "chqk,cqhd->ckhd", grad_scores, query_block, preferred_element_type=F32
        )
        values_grad = jnp.einsum(
            "chqk,cqhd->ckhd", low(softmax_weights), grad_block, preferred_element_type=F32
        )
        return (carried[0] + keys_grad, carried[1] + values_grad), query_grad

    frames = jnp.arange(query.shape[1] // PATCHES, dtype=jnp.int32)
    empty = jnp.zeros(keys.shape, F32)
    (grad_keys, grad_values), grad_query = lax.scan(
        one_block,
        (empty, empty),
        (
            query_blocks(query, 1),
            query_blocks(grad_heads, 1),
            query_blocks(log_total, 2),
            query_blocks(row_delta, 2),
            frames,
        ),
    )
    grad_query = jnp.moveaxis(grad_query, 0, 1).reshape(query.shape)
    return grad_query * score_scale, grad_keys * score_scale, grad_values


def general_body(
    hidden_in,
    noise_level,
    noise_table,
    w_ada,
    b_ada,
    w_qkv,
    b_qkv,
    w_out,
    b_out,
    w_up,
    b_up,
    w_down,
    b_down,
    grad_out,
):
    qkv_w, qkv_b, out_w, out_b, up_w, up_b, down_w, down_b = [
        gather_rows(share)
        for share in (w_qkv, b_qkv, w_out, b_out, w_up, b_up, w_down, b_down)
    ]
    clip_count, patches, model_width = hidden_in.shape
    head_dim = model_width // H
    score_scale = 1.0 / math.sqrt(head_dim)
    head_shape = (clip_count, patches, H, head_dim)
    inputs = hidden_in.astype(F32)
    one_hot, embedded, silu_in, modulation = frame_modulation(
        noise_level, noise_table, w_ada, b_ada
    )
    shift_one, scale_one, gate_one, shift_two, scale_two, gate_two = [
        modulation[:, None, column_block * model_width : (column_block + 1) * model_width]
        for column_block in range(6)
    ]
    normed_one = low(modulate(inputs, shift_one, scale_one))
    qkv_all = dot(normed_one, qkv_w) + qkv_b.astype(F32)
    frame_own = lax.axis_index("seq")
    places = frame_own * patches + jnp.arange(patches, dtype=jnp.int32)
    cosine_local, sine_local = angle_table(places, head_dim)
    cosine_wide = cosine_local[None, :, None, :]
    sine_wide = sine_local[None, :, None, :]
    flat_shape = (clip_count, patches, model_width)

    def turned(block):
        part = qkv_all[..., block * model_width : (block + 1) * model_width]
        return low(rotate(part.reshape(head_shape), cosine_wide, sine_wide)).reshape(flat_shape)

    query = as_heads(to_heads(turned(0)))
    keys = as_heads(to_heads(turned(1)))
    values = as_heads(to_heads(low(qkv_all[..., 2 * model_width :])))
    attended, log_total = attend(query, keys, values, score_scale)
    attended_low = to_tokens(attended.reshape(*attended.shape[:2], -1))
    branch_one = dot(attended_low, out_w) + out_b.astype(F32)
    middle = inputs + gate_one * branch_one
    normed_two = low(modulate(middle, shift_two, scale_two))
    hidden_pre = dot(normed_two, up_w) + up_b.astype(F32)
    hidden_act = low(jax.nn.gelu(hidden_pre, approximate=True))
    branch_two = dot(hidden_act, down_w) + down_b.astype(F32)
    outputs = middle + gate_two * branch_two
    cotangent = grad_out.astype(F32)
    grad_gate_two = jnp.sum(cotangent * branch_two, axis=1)
    grad_branch_two = low(cotangent * gate_two)

    def weight_grad(left, right):
        whole = jnp.einsum("cpi,cpo->io", left, right, preferred_element_type=F32)
        return scatter_rows(low(whole)).astype(F32)

    def bias_grad(grad):
        return scatter_rows(jnp.sum(grad.astype(F32), axis=(0, 1)))

    def back_dot(grad, weight):
        return jnp.einsum("cpo,io->cpi", grad, weight, preferred_element_type=F32)

    grad_down_w = weight_grad(hidden_act, grad_branch_two)
    grad_down_b = bias_grad(grad_branch_two)
    grad_act = back_dot(grad_branch_two, down_w)
    unused, gelu_back = jax.vjp(partial(jax.nn.gelu, approximate=True), hidden_pre)
    grad_pre = low(gelu_back(grad_act)[0])
    grad_up_w = weight_grad(normed_two, grad_pre)
    grad_up_b = bias_grad(grad_pre)
    grad_normed_two = back_dot(grad_pre, up_w)
    unused, norm_two_back = jax.vjp(modulate, middle, shift_two, scale_two)
    grad_middle_norm, grad_shift_two, grad_scale_two = norm_two_back(grad_normed_two)
    grad_middle = cotangent + grad_middle_norm
    grad_gate_one = jnp.sum(grad_middle * branch_one, axis=1)
    grad_branch_one = low(grad_middle * gate_one)
    grad_out_w = weight_grad(attended_low, grad_branch_one)
    grad_out_b = bias_grad(grad_branch_one)
    grad_attended = low(back_dot(grad_branch_one, out_w))
    grad_heads = as_heads(to_heads(grad_attended))
    row_delta = jnp.sum(grad_heads.astype(F32) * attended.astype(F32), axis=-1).transpose(0, 2, 1)
    grad_query, grad_keys, grad_values = attend_back(
        query, keys, values, grad_heads, log_total, row_delta, score_scale
    )

    def home(grad):
        return to_tokens(low(grad).reshape(*grad.shape[:2], -1))

    def unturned(grad):
        wide = home(grad).astype(F32).reshape(head_shape)
        return low(unrotate(wide, cosine_wide, sine_wide)).reshape(flat_shape)

    grad_qkv = jnp.concatenate(
        [unturned(grad_query), unturned(grad_keys), home(grad_values)], axis=-1
    )
    grad_qkv_w = weight_grad(normed_one, grad_qkv)
    grad_qkv_b = bias_grad(grad_qkv)
    grad_normed_one = back_dot(grad_qkv, qkv_w)
    unused, norm_one_back = jax.vjp(modulate, inputs, shift_one, scale_one)
    grad_input_norm, grad_shift_one, grad_scale_one = norm_one_back(grad_normed_one)
    grad_input = grad_middle + grad_input_norm
    grad_modulation = low(
        jnp.concatenate(
            [
                grad_shift_one[:, 0],
                grad_scale_one[:, 0],
                grad_gate_one,
                grad_shift_two[:, 0],
                grad_scale_two[:, 0],
                grad_gate_two,
            ],
            axis=-1,
        )
    )
    grad_table, grad_ada_w, grad_ada_b = frame_gradients(
        grad_modulation, one_hot, embedded, silu_in, w_ada
    )
    return (
        low(outputs),
        low(grad_input),
        grad_table,
        grad_ada_w,
        grad_ada_b,
        grad_qkv_w,
        grad_qkv_b,
        grad_out_w,
        grad_out_b,
        grad_up_w,
        grad_up_b,
        grad_down_w,
        grad_down_b,
    )


def solution(mesh):
    tokens = P("dp", "seq", None)
    matrix = P(ALL, None)
    vector = P(ALL)
    parameters = (matrix,) + (matrix, vector) * 5
    return jax.shard_map(
        general_body,
        mesh=mesh,
        in_specs=(tokens, P("dp", "seq")) + parameters + (tokens,),
        out_specs=(tokens, tokens) + parameters,
        check_vma=False,
    )
```

time: 1860 us -> 1410 us (0.76)
  waiting for transfers between devices: 1160 us -> 672 us
  blocking collectives: 151 us -> 256 us
  matrix products: 266 us -> 179 us
  other arithmetic: 80.5 us -> 120 us
  local copies, waits for them, and re-layouts: 168 us -> 130 us
  starting transfers between devices: 1.38 us -> 32.5 us
    reduce_scatter x6 -> x4, waiting for transfers between devices: 839 us -> 302 us  [scatter_rows(): return lax.psum_scatter(whole, ALL, scatter_dimension=0, tiled=True)]
    all_gather x10 -> x4, waiting for transfers between devices: 325 us -> 71.1 us  [gather_rows(): return lax.all_gather(low(share), ALL, axis=0, tiled=True)]
    unnamed x16 -> x12, waiting for transfers between devices: 0.26 us -> 216 us
    dot_general x43 -> x73, matrix products: 266 us -> 179 us  [the longest x6 26.3 us: dot(): return jnp.dot(left, right, preferred_element_type=F32)]
    all_to_all x0 -> x8, waiting for transfers between devices: none -> 82.5 us  [the longest x4 65.2 us: to_heads(): lax.all_to_all(values, 'seq', split_axis=2, concat_axis=1, tiled=True)]
    all_gather x3, blocking collectives: 69.4 us -> 136 us  [the longest x1 51 us: gather_rows(): return lax.all_gather(low(share), ALL, axis=0, tiled=True)]
    unnamed x7 -> x12, other arithmetic: 0.01 us -> 62.3 us
    another operation x4 -> x2, local copies, waits for them, and re-layouts: 46.4 us -> 8.01 us  [general_body(): attended_low = to_tokens(attended.reshape(*attended.shape[:2], -1))]
  transfers between devices with their start and end apart: 16 -> 18, of which waited for: 12 -> 11; matrix products, arithmetic and copies ran while one was open for 25% -> 18% of each run, Pallas kernels for 0% -> 0%
where the time goes in v1:
time: 1410 us
  waiting for transfers between devices  672 us (48%)
  blocking collectives  256 us (18%)
  matrix products  179 us (13%)
  local copies, waits for them, and re-layouts  130 us (9%)
  other arithmetic  120 us (9%)
  starting transfers between devices  32.5 us (2%)
  between operations  16.5 us (1%)
    reduce_scatter x4, waiting for transfers between devices, scatter_rows(): return lax.psum_scatter(whole, ALL, scatter_dimension=0, tiled=True)  302 us
    unnamed x12, waiting for transfers between devices  216 us
    unnamed x3, blocking collectives  120 us
    all_gather x4, waiting for transfers between devices, gather_rows(): return lax.all_gather(low(share), ALL, axis=0, tiled=True)  71.1 us
    all_to_all x4, waiting for transfers between devices, to_heads(): lax.all_to_all(values, 'seq', split_axis=2, concat_axis=1, tiled=True)  65.2 us
    unnamed x12, other arithmetic  62.3 us
    all_gather x1, blocking collectives, gather_rows(): return lax.all_gather(low(share), ALL, axis=0, tiled=True)  51 us
    all_gather x1, blocking collectives, frame_gradients(): lax.all_gather(silu_back(grad_silu)[0], ALL, axis=1, tiled=True)  43.9 us
  transfers between devices with their start and end apart: 18, of which 11 were waited for; matrix products, arithmetic and copies ran while one was open for 18% of the time, Pallas kernels for 0%

profile of v1, /device:TPU:0, one launch (start us, length us, event | category | flops | bytes accessed | tf_op | source)
XLA Modules:
  0.0 1406.4 jit_solution(11312097935507649103)
XLA Ops:
  8.1 42.0 %all-reduce = s32[32]{0:T(128)S(1)} all-reduce(s32[32]{0:T(128)S(1)} %bitcast_dynamic-update-slice_fusion.1), channel_id=2, replica_groups=mesh['dp'=4,'seq'=8] {'dp','seq'}, use_global_device_ids=true, to_apply=%add | all-reduce | flops 32 | bytes 256
  52.1 133.7 %reduce-scatter.16.cloned.1.call-done = bf16[32,32]{1,0:T(8,128)(2,1)} async-done(((bf16[1024,32]{1,0:T(8,128)(2,1)}), bf16[32,32]{1,0:T(8,128)(2,1)}) %reduce-scatter.16.cloned.1.call-update) | async-done | bytes 2064
  194.2 38.1 %all-reduce.11 = (bf16[3072]{0:T(1024)(128)(2,1)S(1)}, bf16[6144]{0:T(1024)(128)(2,1)S(1)}, bf16[1024]{0:T(1024)(128)(2,1)}, bf16[1024]{0:T(1024)(128)(2,1)}) all-reduce(bf16[3072]{0:T(1024)(128)(2,1)S(1)} %dynamic-update-slice.2, bf16[6144]{0:T(1024)(128)(2,1)S(1)} %dynamic-update-slice.1, ...), channel_id=1, replica_groups=mesh['dp'=4,'seq'=8] {'dp','seq'}, use_global_device_ids=true, to_apply=%add.2 | all-reduce | flops 11264 | bytes 45056
  235.5 82.3 %all-reduce.14.cloned.1.call-done = f32[32,6144]{1,0:T(8,128)} async-done(((f32[32,6144]{1,0:T(8,128)}), f32[32,6144]{1,0:T(8,128)}) %all-reduce.14.cloned.1.call-update) | async-done | bytes 786448
  318.8 71.0 %all-gather.8.cloned.1.call-done = bf16[1024,3072]{1,0:T(8,128)(2,1)} async-done(((bf16[32,3072]{1,0:T(8,128)(2,1)}), bf16[1024,3072]{1,0:T(8,128)(2,1)}) %all-gather.8.cloned.1.call-update) | async-done | bytes 6291472 | tf_op jit(solution)/shard_map/all_gather | solution.py:82
  440.4 13.6 all-to-all-done
  464.5 14.0 all-to-all-done.1
  485.8 22.5 %all-to-all-done.2 = bf16[8,2,16384]{2,1,0:T(2,128)(2,1)S(1)} async-done(((bf16[8,2,16384]{2,1,0:T(2,128)(2,1)}), bf16[8,2,16384]{2,1,0:T(2,128)(2,1)S(1)}, u32[]{:S(2)}, u32[]{:S(2)}) %all-to-all-start.2) | async-done | bytes 524320 | tf_op jit(solution)/shard_map/all_to_all | solution.py:125
  509.6 39.0 %while.31 = (s32[]{:T(128)}, bf16[8,1,256,2,64]{2,4,3,1,0:T(8,128)(2,1)}, f32[8,1,2,256]{3,2,1,0:T(2,128)S(1)}, s32[8]{0:T(128)S(1)}, bf16[8,1,256,2,64]{2,4,3,1...) while((s32[]{:T(128)}, ...), condition=%wide.region_7.8_spmd, body=%wide.region_4.7_spmd.sunk | while | flops 281069056 | bytes 13787257 | solution.py:163
  556.6 12.3 reduce.33
  575.1 51.0 %all-gather.1 = bf16[32,1,128]{2,1,0:T(2,128)(2,1)S(1)} all-gather(bf16[1,1,128]{2,1,0:T(2,128)(2,1)S(1)} %convert_bitcast_fusion.3), channel_id=1, replica_groups=mesh['dp'=4,'seq'=8] {'dp','seq'}, dimensions={0}, use_global_device_ids=true | all-gather | bytes 8448 | tf_op jit(solution)/shard_map/all_gather | solution.py:82
  642.3 12.0 convert_reduce_fusion
  678.3 15.1 %all-to-all-done.4 = bf16[8,2,16384]{2,1,0:T(2,128)(2,1)} async-done(((bf16[8,2,16384]{2,1,0:T(2,128)(2,1)}), bf16[8,2,16384]{2,1,0:T(2,128)(2,1)}, u32[]{:S(2)}, u32[]{:S(2)}) %all-to-all-start.4) | async-done | bytes 524320 | tf_op jit(solution)/shard_map/all_to_all | solution.py:125
  700.3 110.4 %while.32 = (s32[]{:T(128)}, f32[1,2048,2,64]{1,3,2,0:T(8,128)}, f32[1,2048,2,64]{1,3,2,0:T(8,128)}, f32[8,1,256,2,64]{2,4,3,1,0:T(8,128)}, bf16[8,1,256,2,64]{2...) while((s32[]{:T(128)}, f32[1,2048,2,64]{1,3,2,0:T(8,128)}, ...), condition=%wide.region_14.15_spmd.clone, body=%wide.region_13.14_spmd.clone.sunk | while | flops 679495680 | bytes 58609904 | solution.py:188
  812.9 11.5 reduce.35
  834.8 11.5 reduce.36
  853.1 11.5 reduce.37
  878.4 12.7 all-to-all-done.6
  907.0 11.4 concatenate.91
  954.5 40.8 %all-gather.2 = bf16[32,1,6144]{2,1,0:T(2,128)(2,1)S(1)} all-gather(bf16[1,1,6144]{2,1,0:T(2,128)(2,1)S(1)} %bitcast.412), channel_id=1, replica_groups=mesh['dp'=4,'seq'=8] {'dp','seq'}, dimensions={0}, use_global_device_ids=true | all-gather | bytes 405504 | tf_op jit(solution)/shard_map/all_gather | solution.py:105
  998.7 40.0 %all-reduce.10 = (f32[3072]{0:T(1024)S(1)}, f32[1024]{0:T(1024)S(1)}, f32[4096]{0:T(1024)S(1)}, f32[1024]{0:T(1024)S(1)}) all-reduce(f32[3072]{0:T(1024)S(1)} %convert_reduce_fusion.1, f32[1024]{0:T(1024)S(1)} %get-tuple-element.417, f32[4096]{0:T(1024)S(1)} %get-tuple-element.464, ...), channel_id=6, replica_groups=mesh['dp'=4,'seq'=8] {'dp','seq'}, use_global_device_ids=true, to_apply=%region_26.27.clone | all-reduce | flops 9216 | bytes 73728
  1041.8 43.9 %all_gather.47 = f32[32,1024]{0,1:T(8,128)S(1)} all-gather(f32[32,32]{0,1:T(8,128)S(1)} %copy.190), channel_id=1, replica_groups=mesh['dp'=4,'seq'=8] {'dp','seq'}, dimensions={1}, use_global_device_ids=true | all-gather | bytes 135168 | tf_op jit(solution)/shard_map/all_gather | solution.py:117
  1093.6 151.7 %reduce-scatter.12.cloned.1.call-done = bf16[32,4096]{1,0:T(8,128)(2,1)} async-done(((bf16[1024,4096]{1,0:T(8,128)(2,1)}), bf16[32,4096]{1,0:T(8,128)(2,1)}) %reduce-scatter.12.cloned.1.call-update) | async-done | bytes 262160 | tf_op jit(solution)/shard_map/reduce_scatter | solution.py:86
  1247.0 150.5 %reduce-scatter.14.cloned.1.call-done = bf16[128,1024]{1,0:T(8,128)(2,1)} async-done(((bf16[4096,1024]{1,0:T(8,128)(2,1)}), bf16[128,1024]{1,0:T(8,128)(2,1)}) %reduce-scatter.14.cloned.1.call-update) | async-done | bytes 262160 | tf_op jit(solution)/shard_map/reduce_scatter | solution.py:86
  (490 shorter events, 396.0 us)
Async XLA Ops:
  7.2 185.3 %copy-start.25 = (f32[32,4096]{1,0:T(8,128)S(1)}, f32[32,4096]{1,0:T(8,128)}, u32[]{:S(2)}) copy-start(f32[32,4096]{1,0:T(8,128)} %param.27) | copy-start | bytes 1572868
  7.2 186.0 %copy-start.57 = (f32[96]{0:T(128)S(1)}, f32[96]{0:T(128)}, u32[]{:S(2)}) copy-start(f32[96]{0:T(128)} %param.24) | copy-start | bytes 1156
  7.2 186.1 %copy-start.56 = (f32[192]{0:T(256)S(1)}, f32[192]{0:T(256)}, u32[]{:S(2)}) copy-start(f32[192]{0:T(256)} %param.22) | copy-start | bytes 2308
  7.2 186.1 %copy-start.58 = (f32[32]{0:T(128)S(1)}, f32[32]{0:T(128)}, u32[]{:S(2)}) copy-start(f32[32]{0:T(128)} %param.26) | copy-start | bytes 388
  7.2 186.1 %copy-start.59 = (f32[32]{0:T(128)S(1)}, f32[32]{0:T(128)}, u32[]{:S(2)}) copy-start(f32[32]{0:T(128)} %param.30) | copy-start | bytes 388
  7.2 178.6 %reduce-scatter.16.cloned.1.call-start = ((), (), s32[]{:S(2)}) async-start(), calls=%async_computation.21 | async-start | bytes 270336
  8.0 225.0 %copy-start.45 = (s32[32]{0:T(128)}, s32[32]{0:T(128)S(1)}, u32[]{:S(2)}) copy-start(s32[32]{0:T(128)S(1)} %iota_add_fusion.1) | copy-start | bytes 388
  52.1 265.7 %all-reduce.14.cloned.1.call-start = ((), (), s32[]{:S(2)}) async-start(), calls=%async_computation.22 | async-start | bytes 1572864
  189.0 200.9 %all-gather.8.cloned.1.call-start = ((), (), s32[]{:S(2)}) async-start(), calls=%async_computation.13 | async-start | bytes 6488064 | tf_op jit(solution)/shard_map/all_gather | solution.py:82
  190.7 439.8 %all-gather.10.cloned.1.call-start = ((), (), s32[]{:S(2)}) async-start(), calls=%async_computation.14 | async-start | bytes 2162688 | tf_op jit(solution)/shard_map/all_gather | solution.py:82
  192.4 442.0 %all-gather.12.cloned.1.call-start = ((), (), s32[]{:S(2)}) async-start(), calls=%async_computation.15 | async-start | bytes 8650752 | tf_op jit(solution)/shard_map/all_gather | solution.py:82
  431.2 22.9 %all-to-all-start = ((bf16[8,2,16384]{2,1,0:T(2,128)(2,1)}), bf16[8,2,16384]{2,1,0:T(2,128)(2,1)S(1)}, u32[]{:S(2)}, u32[]{:S(2)}) async-start(bf16[8,2,16384]{2,1,0:T(2,128)(2,1)} %reshape.1247), calls=%async_computation | async-start | bytes 1048576 | tf_op jit(solution)/shard_map/all_to_all | solution.py:125
  454.0 24.4 %all-to-all-start.1 = ((bf16[8,2,16384]{2,1,0:T(2,128)(2,1)}), bf16[8,2,16384]{2,1,0:T(2,128)(2,1)S(1)}, u32[]{:S(2)}, u32[]{:S(2)}) async-start(bf16[8,2,16384]{2,1,0:T(2,128)(2,1)} %reshape.1249), calls=%async_computation.1 | async-start | bytes 1048576 | tf_op jit(solution)/shard_map/all_to_all | solution.py:125
  478.4 30.0 %all-to-all-start.2 = ((bf16[8,2,16384]{2,1,0:T(2,128)(2,1)}), bf16[8,2,16384]{2,1,0:T(2,128)(2,1)S(1)}, u32[]{:S(2)}, u32[]{:S(2)}) async-start(bf16[8,2,16384]{2,1,0:T(2,128)(2,1)} %reshape.1251), calls=%async_computation.2 | async-start | bytes 1048576 | tf_op jit(solution)/shard_map/all_to_all | solution.py:125
  481.9 160.3 %all-gather.14.cloned.1.call-start = ((), (), s32[]{:S(2)}) async-start(), calls=%async_computation.16 | async-start | bytes 8650752 | tf_op jit(solution)/shard_map/all_gather | solution.py:82
  570.9 55.3 %all-to-all-start.3 = ((bf16[8,2,16384]{2,1,0:T(2,128)(2,1)}), bf16[8,2,16384]{2,1,0:T(2,128)(2,1)}, u32[]{:S(2)}, u32[]{:S(2)}) async-start(bf16[8,2,16384]{2,1,0:T(2,128)(2,1)} %reshape.1253), calls=%async_computation.3 | async-start | bytes 1048576 | tf_op jit(solution)/shard_map/all_to_all | solution.py:129
  673.7 19.7 %all-to-all-start.4 = ((bf16[8,2,16384]{2,1,0:T(2,128)(2,1)}), bf16[8,2,16384]{2,1,0:T(2,128)(2,1)}, u32[]{:S(2)}, u32[]{:S(2)}) async-start(bf16[8,2,16384]{2,1,0:T(2,128)(2,1)} %reshape.1255), calls=%async_computation.4 | async-start | bytes 1048576 | tf_op jit(solution)/shard_map/all_to_all | solution.py:125
  825.4 21.9 %all-to-all-start.7 = ((bf16[8,2,16384]{2,1,0:T(2,128)(2,1)}), bf16[8,2,16384]{2,1,0:T(2,128)(2,1)}, u32[]{:S(2)}, u32[]{:S(2)}) async-start(bf16[8,2,16384]{2,1,0:T(2,128)(2,1)} %reshape.1257), calls=%async_computation.7 | async-start | bytes 1048576 | tf_op jit(solution)/shard_map/all_to_all | solution.py:129
  829.5 260.8 %reduce-scatter.10.cloned.1.call-start = ((), (), s32[]{:S(2)}) async-start(), calls=%async_computation.18 | async-start | bytes 2162688 | tf_op jit(solution)/shard_map/reduce_scatter | solution.py:86
  847.3 22.8 %all-to-all-start.5 = ((bf16[8,2,16384]{2,1,0:T(2,128)(2,1)}), bf16[8,2,16384]{2,1,0:T(2,128)(2,1)S(1)}, u32[]{:S(2)}, u32[]{:S(2)}) async-start(bf16[8,2,16384]{2,1,0:T(2,128)(2,1)} %reshape.1261), calls=%async_computation.5 | async-start | bytes 1048576 | tf_op jit(solution)/shard_map/all_to_all | solution.py:129
  870.1 21.0 %all-to-all-start.6 = ((bf16[8,2,16384]{2,1,0:T(2,128)(2,1)}), bf16[8,2,16384]{2,1,0:T(2,128)(2,1)S(1)}, u32[]{:S(2)}, u32[]{:S(2)}) async-start(bf16[8,2,16384]{2,1,0:T(2,128)(2,1)} %reshape.1259), calls=%async_computation.6 | async-start | bytes 1048576 | tf_op jit(solution)/shard_map/all_to_all | solution.py:129
  873.6 218.3 %reduce-scatter.8.cloned.1.call-start = ((), (), s32[]{:S(2)}) async-start(), calls=%async_computation.17 | async-start | bytes 6488064 | tf_op jit(solution)/shard_map/reduce_scatter | solution.py:86
  926.0 319.3 %reduce-scatter.12.cloned.1.call-start = ((), (), s32[]{:S(2)}) async-start(), calls=%async_computation.19 | async-start | bytes 8650752 | tf_op jit(solution)/shard_map/reduce_scatter | solution.py:86
  934.6 463.0 %reduce-scatter.14.cloned.1.call-start = ((), (), s32[]{:S(2)}) async-start(), calls=%async_computation.20 | async-start | bytes 8650752 | tf_op jit(solution)/shard_map/reduce_scatter | solution.py:86
  (69 other events, 2256.4 us)
Sparse Core Ops, SparseCore 0:
  52.2 133.6 reduce-scatter.15
  192.5 125.2 all-reduce.13
  321.4 68.4 all-gather.7
  393.2 55.9 all-gather.9
  452.7 89.7 all-gather.11
  545.9 83.4 all-gather.13
  832.6 139.6 reduce-scatter.9
  978.9 112.9 reduce-scatter.7
  1094.2 151.0 reduce-scatter.11
  1247.4 150.0 reduce-scatter.13

commit v2 on v1

--- a/solution.py
+++ b/solution.py
@@ -4,6 +4,8 @@
 import jax
 import jax.numpy as jnp
 from jax import lax
+from jax.experimental import pallas as pl
+from jax.experimental.pallas import tpu as pltpu
 from jax.sharding import PartitionSpec as P
 
 H = 16
@@ -342,13 +344,736 @@
     )
 
 
+MESH_ID = pl.DeviceIdType.MESH
+VMEM_LIMIT = 60 * 1024 * 1024
+HEADS_WIDE = 128
+
+
+def contract(left, right, left_dim, right_dim, precision=None):
+    return lax.dot_general(
+        left,
+        right,
+        (((left_dim,), (right_dim,)), ((), ())),
+        preferred_element_type=F32,
+        precision=precision,
+    )
+
+
+class Place:
+    def __init__(self):
+        self.dp = lax.axis_index("dp")
+        self.seq = lax.axis_index("seq")
+        self.z = self.seq // 2
+        self.core = self.seq % 2
+        self.other = 1 - self.core
+        self.x_dp = self.dp + 1 - 2 * (self.dp % 2)
+        self.y_dp = (self.dp + 2) % 4
+        self.far_dp = 3 - self.dp
+        self.dp_peers = (self.x_dp, self.y_dp, self.far_dp)
+        self.seq_peers = [(self.seq + step) % 8 for step in range(1, 8)]
+        self.sibling = (self.dp, self.z * 2 + self.other)
+
+    def at_dp(self, dp):
+        return (dp, self.seq)
+
+    def at_seq(self, seq):
+        return (self.dp, seq)
+
+    def greet(self):
+        barrier = pltpu.get_barrier_semaphore()
+        peers = [self.at_dp(dp) for dp in self.dp_peers]
+        peers += [self.at_seq(seq) for seq in self.seq_peers]
+        for peer in peers:
+            pl.semaphore_signal(barrier, inc=1, device_id=peer, device_id_type=MESH_ID)
+        pl.semaphore_wait(barrier, len(peers))
+
+
+class Wire:
+    def __init__(self, send_sems, recv_sems):
+        self.send_sems = send_sems
+        self.recv_sems = recv_sems
+        self.used = 0
+        self.sent = []
+
+    def send(self, source, target, device):
+        copy = pltpu.make_async_remote_copy(
+            src_ref=source,
+            dst_ref=target,
+            send_sem=self.send_sems.at[self.used],
+            recv_sem=self.recv_sems.at[self.used],
+            device_id=device,
+            device_id_type=MESH_ID,
+        )
+        self.used += 1
+        copy.start()
+        self.sent.append(copy)
+        return copy
+
+    def drain(self):
+        for copy in self.sent:
+            copy.wait_send()
+        self.sent = []
+
+
+def arrive(copies):
+    for copy in copies:
+        copy.wait_recv()
+
+
+class Gather:
+    def __init__(self, wire, place, ref):
+        self.wire, self.place, self.ref = wire, place, ref
+
+    def along_z(self):
+        place, ref = self.place, self.ref
+        own = ref.at[place.dp, place.z, place.core]
+        self.coming = [
+            self.wire.send(own, own, place.at_seq(((place.z + step) % 4) * 2 + place.core))
+            for step in (1, 2, 3)
+        ]
+
+    def along_xy(self):
+        place = self.place
+        arrive(self.coming)
+        own = self.ref.at[place.dp, :, place.core]
+        self.coming = [
+            self.wire.send(own, own, place.at_dp(dp)) for dp in (place.x_dp, place.y_dp)
+        ]
+
+    def across(self):
+        place = self.place
+        arrive(self.coming)
+        from_x = self.ref.at[place.x_dp, pl.ds(0, 2), place.core]
+        from_y = self.ref.at[place.y_dp, pl.ds(2, 2), place.core]
+        self.coming = [
+            self.wire.send(from_x, from_x, place.at_dp(place.y_dp)),
+            self.wire.send(from_y, from_y, place.at_dp(place.x_dp)),
+        ]
+
+    def to_sibling(self):
+        place = self.place
+        arrive(self.coming)
+        mine = self.ref.at[:, :, place.core]
+        self.coming = [self.wire.send(mine, mine, place.sibling)]
+
+    def finish(self):
+        arrive(self.coming)
+
+
+class SmallGather:
+    def __init__(self, wire, place, ref):
+        self.wire, self.place, self.ref = wire, place, ref
+
+    def along_seq(self):
+        place = self.place
+        own = self.ref.at[place.dp, place.seq]
+        self.coming = [self.wire.send(own, own, place.at_seq(seq)) for seq in place.seq_peers]
+
+    def along_dp(self):
+        place = self.place
+        arrive(self.coming)
+        own = self.ref.at[place.dp]
+        self.coming = [self.wire.send(own, own, place.at_dp(dp)) for dp in place.dp_peers]
+
+    def finish(self):
+        arrive(self.coming)
+
+
+def spread_dp(wire, place, part_of, slots):
+    return [
+        wire.send(part_of(dp), slots.at[index], place.at_dp(dp))
+        for index, dp in enumerate(place.dp_peers)
+    ]
+
+
+def spread_seq(wire, place, part_of, slots):
+    return [
+        wire.send(part_of(seq), slots.at[index], place.at_seq(seq))
+        for index, seq in enumerate(place.seq_peers)
+    ]
+
+
+def total_of(own, slots, count):
+    total = own
+    for index in range(count):
+        total = total + slots[index].astype(F32)
+    return total
+
+
+def row_of(lines, first):
+    return jnp.concatenate([lines[first + line : first + line + 1, :] for line in range(8)], axis=1)
+
+
+def lines_of(row):
+    return jnp.concatenate([row[:, 128 * line : 128 * (line + 1)] for line in range(8)], axis=0)
+
+
+def whole_piece(piece):
+    value = piece[...]
+    return value.reshape(-1, value.shape[-1])
+
+
+def norm_parts(values):
+    centred = values - jnp.mean(values, axis=1, keepdims=True)
+    inverse = lax.rsqrt(jnp.mean(centred * centred, axis=1, keepdims=True) + norm_eps)
+    return centred * inverse, inverse
+
+
+def half_turn(values):
+    lane = lax.broadcasted_iota(jnp.int32, values.shape, 1) % 64
+    in_time = lane < 16
+    first = (lane < 8) | ((lane >= 16) & (lane < 28)) | ((lane >= 40) & (lane < 52))
+    up = jnp.where(in_time, pltpu.roll(values, 120, 1), pltpu.roll(values, 116, 1))
+    down = jnp.where(in_time, pltpu.roll(values, 8, 1), pltpu.roll(values, 12, 1))
+    return jnp.where(first, up, down)
+
+
+def split_heads(values):
+    lane = lax.broadcasted_iota(jnp.int32, values.shape, 1)
+    empty = jnp.zeros_like(values)
+    return jnp.concatenate(
+        [jnp.where(lane < 64, values, empty), jnp.where(lane < 64, empty, values)], axis=0
+    )
+
+
+def join_heads(turned):
+    return jnp.concatenate([turned[:64, :256], turned[64:, 256:]], axis=0).T
+
+
+def attend_frame(frame, query, keys, values, attended, log_total, scores):
+    pair = split_heads(query[frame])
+    row_max = None
+    for block in range(frame + 1):
+        block_scores = contract(keys[block], pair, 1, 1)
+        scores[block] = block_scores
+        block_max = jnp.max(block_scores, axis=0, keepdims=True)
+        row_max = block_max if row_max is None else jnp.maximum(row_max, block_max)
+    row_total = None
+    weighted = None
+    for block in range(frame + 1):
+        exponent = jnp.exp(scores[block] - row_max)
+        block_total = jnp.sum(exponent, axis=0, keepdims=True)
+        block_sum = contract(values[block], exponent.astype(BF16), 0, 0)
+        row_total = block_total if row_total is None else row_total + block_total
+        weighted = block_sum if weighted is None else weighted + block_sum
+    attended[frame] = join_heads(weighted / row_total).astype(BF16)
+    log_total[frame] = row_max + jnp.log(row_total)
+
+
+SQRT_TWO_OVER_PI = math.sqrt(2.0 / math.pi)
+
+
+def gelu_parts(values):
+    square = values * values
+    bent = jnp.tanh(SQRT_TWO_OVER_PI * values * (1.0 + 0.044715 * square))
+    half = 0.5 * (1.0 + bent)
+    slope = half + 0.5 * values * (1.0 - bent * bent) * (
+        SQRT_TWO_OVER_PI * (1.0 + 3.0 * 0.044715 * square)
+    )
+    return values * half, slope
+
+
+def forward_kernel(
+    x_ref,
+    cotangent_ref,
+    level_ref,
+    table_ref,
+    w_ada_ref,
+    bias_ref,
+    w_qkv_ref,
+    w_out_ref,
+    w_up_ref,
+    w_down_ref,
+    cosine_ref,
+    sine_ref,
+    layer_out_ref,
+    wide_out,
+    down_out,
+    query_ref,
+    keys_ref,
+    values_ref,
+    attended_ref,
+    log_total_ref,
+    attended_tokens,
+    normed_one_ref,
+    normed_two_ref,
+    middle_ref,
+    branch_one_ref,
+    act_ref,
+    slope_ref,
+    modulation_ref,
+    embedded_ref,
+    one_hot_ref,
+    gate_two_grad_ref,
+    wide,
+    down,
+    levels,
+    found,
+    found_dp,
+    found_sum,
+    found_seq,
+    partial_mod,
+    mod_dp,
+    mod_sum,
+    mod_blocks,
+    mod_seq,
+    bias_dp,
+    bias_sum,
+    bias_seq,
+    flat,
+    scores,
+    send_sems,
+    recv_sems,
+    back_send,
+    back_recv,
+    local_sems,
+):
+    place = Place()
+    wire = Wire(send_sems, recv_sems)
+    dp, seq, z, core = place.dp, place.seq, place.z, place.core
+    device = dp * 8 + seq
+    levels[dp, seq] = level_ref[...]
+    for block in range(3):
+        wide[block, dp, z, core] = low(w_qkv_ref[:, 1024 * block : 1024 * (block + 1)])
+    place.greet()
+    level_gather = SmallGather(wire, place, levels)
+    level_gather.along_seq()
+    pieces = [Gather(wire, place, wide.at[index]) for index in range(8)]
+    pieces += [Gather(wire, place, down.at[index]) for index in range(4)]
+    pieces[0].along_z()
+    pieces[1].along_z()
+    bias_copies = spread_dp(wire, place, lambda dp: bias_ref, bias_dp)
+    wide[3, dp, z, core] = low(w_out_ref[...])
+    for block in range(4):
+        wide[4 + block, dp, z, core] = low(w_up_ref[:, 1024 * block : 1024 * (block + 1)])
+    for block in range(4):
+        down[block, dp, z, core] = low(w_down_ref[:, 256 * block : 256 * (block + 1)])
+    pieces[2].along_z()
+    saved = []
+
+    def save(index):
+        pieces[index].finish()
+        source, target = (
+            (wide.at[index], wide_out.at[index])
+            if index < 8
+            else (down.at[index - 8], down_out.at[index - 8])
+        )
+        copy = pltpu.make_async_copy(source, target, local_sems.at[index])
+        copy.start()
+        saved.append(copy)
+
+    def tick(step, finish=True):
+        if step + 2 < 12 and step > 0:
+            pieces[step + 2].along_z()
+        if step < 12:
+            pieces[step].along_xy()
+        if 0 <= step - 1 < 12:
+            pieces[step - 1].across()
+        if 0 <= step - 2 < 12:
+            pieces[step - 2].to_sibling()
+        if finish and 0 <= step - 3 < 12:
+            save(step - 3)
+
+    level_gather.along_dp()
+    x = x_ref[...].astype(F32)
+    normed, unused = norm_parts(x)
+    flat[0] = normed
+    level_gather.finish()
+    level_rows = jnp.concatenate(
+        [levels[group, frame, 0:1, :] for group in range(4) for frame in range(8)]
+        + [jnp.full((96, 128), -1.0, F32)],
+        axis=0,
+    )
+    lane = lax.broadcasted_iota(jnp.int32, (128, 128), 1)
+    own_level = (lane + device * 32).astype(F32)
+    one_hot = jnp.where((level_rows == own_level) & (lane < 32), 1.0, 0.0)
+    one_hot_ref[...] = one_hot
+    one_hot_turned = low(one_hot.T)[:32, :]
+    found[...] = low(contract(low(table_ref[...]), one_hot_turned, 0, 0)).reshape(found.shape)
+    found_copies = spread_dp(wire, place, lambda dp: found.at[dp], found_dp)
+    pieces[0].along_xy()
+    arrive(found_copies)
+    found_sum[...] = low(total_of(found[dp].astype(F32), found_dp, 3))
+    found_copies = spread_seq(wire, place, lambda seq: found_sum.at[seq], found_seq)
+    tick(1)
+    arrive(found_copies)
+    embedded = total_of(found_sum[seq].astype(F32), found_seq, 7)
+    embedded_ref[...] = embedded
+    silu_in = low(embedded / (1.0 + jnp.exp(-embedded)))
+    for block in range(6):
+        part = contract(silu_in, low(w_ada_ref[:, 1024 * block : 1024 * (block + 1)]), 0, 0)
+        for line in range(8):
+            partial_mod[8 * block + line] = part[:32, 128 * line : 128 * (line + 1)].reshape(
+                4, 8, 128
+            )
+    mod_copies = spread_dp(wire, place, lambda dp: partial_mod.at[:, dp], mod_dp)
+    arrive(bias_copies)
+    bias_sum[...] = low(total_of(bias_ref[...].astype(F32), bias_dp, 3))
+    bias_copies = spread_seq(wire, place, lambda seq: bias_sum, bias_seq)
+    tick(2)
+    arrive(mod_copies)
+    mod_sum[...] = total_of(partial_mod[:, dp], mod_dp, 3).reshape(384, 128)
+    for frame in range(8):
+        mod_blocks[frame] = mod_sum[pl.ds(frame, 48, stride=8), :]
+    mod_copies = spread_seq(wire, place, lambda seq: mod_blocks.at[seq], mod_seq)
+    tick(3)
+    arrive(bias_copies)
+    biases = total_of(bias_sum[...].astype(F32), bias_seq, 7)
+    arrive(mod_copies)
+    modulation = total_of(mod_blocks[seq], mod_seq, 7) + biases[72:120]
+    for block in range(6):
+        modulation_ref[block : block + 1, :] = row_of(modulation, 8 * block)
+    shift_one = modulation_ref[0:1, :]
+    scale_one = modulation_ref[1:2, :]
+    gate_one = modulation_ref[2:3, :]
+    shift_two = modulation_ref[3:4, :]
+    scale_two = modulation_ref[4:5, :]
+    gate_two = modulation_ref[5:6, :]
+    normed_one_ref[...] = low(flat[0] * (1.0 + scale_one) + shift_one)
+    cosine = cosine_ref[...]
+    sine = sine_ref[...]
+    head_copies = []
+
+    def project(block, target):
+        r = contract(normed_one_ref[...], whole_piece(wide.at[block]), 1, 0)
+        r = r + row_of(biases, 8 * block)
+        for group in range(8):
+            part = r[:, 128 * group : 128 * (group + 1)]
+            if block < 2:
+                part = part * cosine + half_turn(part) * sine
+            if block == 0:
+                part = part * 0.125
+            act_ref[:, 1024 * block + 128 * group : 1024 * block + 128 * (group + 1)] = low(part)
+        for other in place.seq_peers:
+            columns = pl.ds(pl.multiple_of(1024 * block + other * 128, 128), 128)
+            head_copies.append(
+                wire.send(act_ref.at[:, columns], target.at[seq], place.at_seq(other))
+            )
+        columns = pl.ds(pl.multiple_of(1024 * block + seq * 128, 128), 128)
+        target[seq] = act_ref[:, columns]
+
+    project(0, query_ref)
+    tick(4)
+    project(1, keys_ref)
+    tick(5)
+    project(2, values_ref)
+    tick(6)
+    arrive(head_copies)
+    back_copies = []
+
+    def send_back(frame):
+        columns = pl.ds(pl.multiple_of(seq * 128, 128), 128)
+
+        @pl.when(seq != frame)
+        def _():
+            pltpu.make_async_remote_copy(
+                src_ref=attended_ref.at[frame],
+                dst_ref=attended_tokens.at[:, columns],
+                send_sem=back_send.at[frame],
+                recv_sem=back_recv.at[seq],
+                device_id=place.at_seq(frame),
+                device_id_type=MESH_ID,
+            ).start()
+
+        @pl.when(seq == frame)
+        def _():
+            attended_tokens[:, columns] = attended_ref[frame]
+
+    def back_copy(other):
+        columns = pl.ds(pl.multiple_of(other * 128, 128), 128)
+        return pltpu.make_async_remote_copy(
+            src_ref=attended_ref.at[other],
+            dst_ref=attended_tokens.at[:, columns],
+            send_sem=back_send.at[other],
+            recv_sem=back_recv.at[other],
+            device_id=place.at_seq(other),
+            device_id_type=MESH_ID,
+        )
+
+    for frame in range(8):
+        attend_frame(
+            frame, query_ref, keys_ref, values_ref, attended_ref, log_total_ref, scores
+        )
+        send_back(frame)
+        if frame in (2, 5):
+            tick(7 if frame == 2 else 8)
+    tick(9)
+    for other in place.seq_peers:
+        back_copy(other).wait_recv()
+    for other in place.seq_peers:
+        back_copy(other).wait_send()
+    for copy in head_copies:
+        copy.wait_send()
+    wire.sent = [copy for copy in wire.sent if not any(copy is done for done in head_copies)]
+    branch_one = contract(attended_tokens[...], whole_piece(wide.at[3]), 1, 0)
+    branch_one = branch_one + row_of(biases, 24)
+    branch_one_ref[...] = branch_one
+    middle = x_ref[...].astype(F32) + gate_one * branch_one
+    middle_ref[...] = middle
+    normed, unused = norm_parts(middle)
+    normed_two_ref[...] = low(normed * (1.0 + scale_two) + shift_two)
+    for block in range(4):
+        if block == 3:
+            tick(10)
+        pre = contract(normed_two_ref[...], whole_piece(wide.at[4 + block]), 1, 0)
+        act, slope = gelu_parts(pre + row_of(biases, 32 + 8 * block))
+        act_ref[:, 1024 * block : 1024 * (block + 1)] = low(act)
+        slope_ref[:, 1024 * block : 1024 * (block + 1)] = low(slope)
+    for block in range(4):
+        tick(11 + block)
+        flat[0, :, 256 * block : 256 * (block + 1)] = contract(
+            act_ref[...], whole_piece(down.at[block]), 1, 0
+        )
+    branch_two = flat[0] + row_of(biases, 64)
+    layer_out_ref[...] = low(middle_ref[...] + gate_two * branch_two)
+    gate_two_grad_ref[...] = jnp.sum(
+        cotangent_ref[...].astype(F32) * branch_two, axis=0, keepdims=True
+    )
+    wire.drain()
+    for copy in saved:
+        copy.wait()
+
+
+def vmem(shape, dtype=F32):
+    return pltpu.VMEM(shape, dtype)
+
+
+def run_forward(x, cotangent, level, table, w_ada, biases, w_qkv, w_out, w_up, w_down, cosine, sine):
+    shape = jax.ShapeDtypeStruct
+    heads = shape((8, 256, 128), BF16)
+    outs = [
+        ((256, 1024), BF16),
+        ((8, 4, 4, 2, 32, 1024), BF16),
+        ((4, 4, 4, 2, 128, 256), BF16),
+        ((8, 256, 128), BF16),
+        ((8, 256, 128), BF16),
+        ((8, 256, 128), BF16),
+        ((8, 256, 128), BF16),
+        ((8, 1, 512), F32),
+        ((256, 1024), BF16),
+        ((256, 1024), BF16),
+        ((256, 1024), BF16),
+        ((256, 1024), F32),
+        ((256, 1024), F32),
+        ((256, 4096), BF16),
+        ((256, 4096), BF16),
+        ((8, 1024), F32),
+        ((32, 128), F32),
+        ((128, 128), F32),
+        ((1, 1024), F32),
+    ]
+    in_vmem = pl.BlockSpec(memory_space=pltpu.VMEM)
+    anywhere = pl.BlockSpec(memory_space=pl.ANY)
+    scratch = [
+        vmem((8, 4, 4, 2, 32, 1024), BF16),
+        vmem((4, 4, 4, 2, 128, 256), BF16),
+        vmem((4, 8, 8, 128)),
+        vmem((4, 8, 32, 128), BF16),
+        vmem((3, 8, 32, 128), BF16),
+        vmem((8, 32, 128), BF16),
+        vmem((7, 32, 128), BF16),
+        vmem((48, 4, 8, 128)),
+        vmem((3, 48, 8, 128)),
+        vmem((384, 128)),
+        vmem((8, 48, 128)),
+        vmem((7, 48, 128)),
+        vmem((3, 128, 128), BF16),
+        vmem((128, 128), BF16),
+        vmem((7, 128, 128), BF16),
+        vmem((1, 256, 1024)),
+        vmem((8, 256, 512)),
+        pltpu.SemaphoreType.DMA((170,)),
+        pltpu.SemaphoreType.DMA((170,)),
+        pltpu.SemaphoreType.DMA((8,)),
+        pltpu.SemaphoreType.DMA((8,)),
+        pltpu.SemaphoreType.DMA((12,)),
+    ]
+    return pl.pallas_call(
+        forward_kernel,
+        out_shape=[shape(*out) for out in outs],
+        in_specs=[in_vmem] * 12,
+        out_specs=[in_vmem, anywhere, anywhere] + [in_vmem] * 16,
+        scratch_shapes=scratch,
+        compiler_params=pltpu.CompilerParams(
+            collective_id=0, has_side_effects=True, vmem_limit_bytes=VMEM_LIMIT
+        ),
+        name="block_forward",
+    )(x, cotangent, level, table, w_ada, biases, w_qkv, w_out, w_up, w_down, cosine, sine)
+
+
+def rope_tables(head_dim):
+    places = lax.axis_index("seq") * PATCHES + jnp.arange(PATCHES, dtype=jnp.int32)
+    cosine, sine = angle_table(places, head_dim)
+    lane = jnp.arange(head_dim)
+    first = jnp.where(lane < 16, lane < 8, (lane - 16) % 24 < 12)
+    sine = jnp.where(first, -sine, sine)
+    return jnp.tile(cosine, (1, 2)), jnp.tile(sine, (1, 2))
+
+
+def own_biases(shares):
+    device = lax.axis_index("dp") * 8 + lax.axis_index("seq")
+    parts = []
+    for share in shares:
+        whole = jnp.zeros((32,) + share.shape, BF16)
+        parts.append(lax.dynamic_update_slice(whole, low(share)[None], (device, 0)).reshape(-1))
+    lines = jnp.concatenate(parts).reshape(-1, 128)
+    return jnp.pad(lines, ((0, 128 - lines.shape[0]), (0, 0)))
+
+
+def fast_body(
+    hidden_in,
+    noise_level,
+    noise_table,
+    w_ada,
+    b_ada,
+    w_qkv,
+    b_qkv,
+    w_out,
+    b_out,
+    w_up,
+    b_up,
+    w_down,
+    b_down,
+    grad_out,
+):
+    cosine, sine = rope_tables(64)
+    level = jnp.broadcast_to(noise_level.astype(F32), (8, 128))
+    biases = own_biases((b_qkv, b_out, b_up, b_down, b_ada))
+    (
+        layer_out,
+        wide,
+        down,
+        query,
+        keys,
+        values,
+        attended,
+        log_total,
+        attended_tokens,
+        normed_one,
+        normed_two,
+        middle,
+        branch_one,
+        act,
+        slope,
+        modulation,
+        embedded,
+        one_hot,
+        grad_gate_two,
+    ) = run_forward(
+        hidden_in[0],
+        grad_out[0],
+        level,
+        noise_table,
+        w_ada,
+        biases,
+        w_qkv,
+        w_out,
+        w_up,
+        w_down,
+        cosine,
+        sine,
+    )
+    wide = wide.reshape(8, 1024, 1024)
+    down = down.reshape(4, 4096, 256)
+    shift_one, scale_one, gate_one, shift_two, scale_two, gate_two = [
+        modulation[block : block + 1] for block in range(6)
+    ]
+    cotangent = grad_out[0].astype(F32)
+    grad_branch_two = low(cotangent * gate_two)
+
+    def weight_grad(left, right):
+        return scatter_rows(low(contract(left, right, 0, 0))).astype(F32)
+
+    def bias_grad(grad):
+        return scatter_rows(jnp.sum(grad.astype(F32), axis=0))
+
+    down_flat = down.transpose(1, 0, 2).reshape(4096, 1024)
+    up_flat = wide[4:].transpose(1, 0, 2).reshape(1024, 4096)
+    qkv_flat = wide[:3].transpose(1, 0, 2).reshape(1024, 3072)
+    grad_down_w = weight_grad(act, grad_branch_two)
+    grad_pre = low(contract(grad_branch_two, down_flat, 1, 1) * slope.astype(F32))
+    grad_up_w = weight_grad(normed_two, grad_pre)
+    grad_normed_two = contract(grad_pre, up_flat, 1, 1)
+    unused, norm_two_back = jax.vjp(modulate, middle, shift_two, scale_two)
+    grad_middle_norm, grad_shift_two, grad_scale_two = norm_two_back(grad_normed_two)
+    grad_middle = cotangent + grad_middle_norm
+    grad_gate_one = jnp.sum(grad_middle * branch_one, axis=0, keepdims=True)
+    grad_branch_one = low(grad_middle * gate_one)
+    grad_out_w = weight_grad(attended_tokens, grad_branch_one)
+    grad_attended = low(contract(grad_branch_one, wide[3], 1, 1))
+    grad_heads = to_heads(grad_attended[None])
+
+    def headed(piece):
+        return piece.reshape(1, 2048, 2, 64)
+
+    row_delta = jnp.sum(
+        headed(grad_heads).astype(F32) * headed(attended).astype(F32), axis=-1
+    ).transpose(0, 2, 1)
+    totals = log_total.reshape(8, 2, 256).transpose(1, 0, 2).reshape(1, 2, 2048)
+    gradients = attend_back(
+        headed(query), headed(keys), headed(values), headed(grad_heads), totals, row_delta, 1.0
+    )
+    grad_query, grad_keys, grad_values = [
+        to_tokens(low(grad).reshape(1, 2048, 128))[0].astype(F32) for grad in gradients
+    ]
+    wide_cosine, wide_sine = jnp.tile(cosine, (1, 8)), jnp.tile(sine, (1, 8))
+
+    def unturned(grad):
+        lane = jnp.arange(1024) % 64
+        first = (lane < 8) | ((lane >= 16) & (lane < 28)) | ((lane >= 40) & (lane < 52))
+        up = jnp.where(lane < 16, jnp.roll(grad, -8, 1), jnp.roll(grad, -12, 1))
+        back = jnp.where(lane < 16, jnp.roll(grad, 8, 1), jnp.roll(grad, 12, 1))
+        return low(grad * wide_cosine - jnp.where(first, up, back) * wide_sine)
+
+    grad_qkv = jnp.concatenate(
+        [unturned(grad_query * 0.125), unturned(grad_keys), low(grad_values)], axis=1
+    )
+    grad_qkv_w = weight_grad(normed_one, grad_qkv)
+    grad_normed_one = contract(grad_qkv, qkv_flat, 1, 1)
+    unused, norm_one_back = jax.vjp(modulate, hidden_in[0].astype(F32), shift_one, scale_one)
+    grad_input_norm, grad_shift_one, grad_scale_one = norm_one_back(grad_normed_one)
+    grad_modulation = low(
+        jnp.concatenate(
+            [
+                grad_shift_one,
+                grad_scale_one,
+                grad_gate_one,
+                grad_shift_two,
+                grad_scale_two,
+                grad_gate_two,
+            ],
+            axis=1,
+        )
+    )
+    columns = embedded[:, :32].T
+    grad_table, grad_ada_w, grad_ada_b = frame_gradients(
+        grad_modulation, one_hot[:32, :32], columns, low(jax.nn.silu(columns)), w_ada
+    )
+    return (
+        layer_out[None],
+        low(grad_middle + grad_input_norm)[None],
+        grad_table,
+        grad_ada_w,
+        grad_ada_b,
+        grad_qkv_w,
+        bias_grad(grad_qkv),
+        grad_out_w,
+        bias_grad(grad_branch_one),
+        grad_up_w,
+        bias_grad(grad_pre),
+        grad_down_w,
+        bias_grad(grad_branch_two),
+    )
+
+
 def solution(mesh):
     tokens = P("dp", "seq", None)
     matrix = P(ALL, None)
     vector = P(ALL)
     parameters = (matrix,) + (matrix, vector) * 5
+    chips = dict(mesh.shape) == {"dp": 4, "seq": 8}
     return jax.shard_map(
-        general_body,
+        fast_body if chips else general_body,
         mesh=mesh,
         in_specs=(tokens, P("dp", "seq")) + parameters + (tokens,),
         out_specs=(tokens, tokens) + parameters,

time: 1410 us -> 985 us (0.70)
  waiting for transfers between devices: 672 us -> 368 us
  Pallas kernels: 0 us -> 163 us
  blocking collectives: 256 us -> 123 us
  matrix products: 179 us -> 120 us
  other arithmetic: 120 us -> 64.9 us
  local copies, waits for them, and re-layouts: 130 us -> 96.7 us
    unnamed x12 -> x4, waiting for transfers between devices: 216 us -> 0.07 us
    pallas_call x0 -> x1, Pallas kernels: none -> 163 us  [run_forward(): pl.pallas_call(forward_kernel, out_shape=[shape(*out) for out in outs], i...]
    unnamed x3 -> x1, blocking collectives: 120 us -> 37.6 us
    all_gather x4 -> x0, waiting for transfers between devices: 71.1 us -> none  [gather_rows(): return lax.all_gather(low(share), ALL, axis=0, tiled=True)]
    all_to_all x4 -> x1, waiting for transfers between devices: 65.2 us -> 12.1 us  [to_heads(): lax.all_to_all(values, 'seq', split_axis=2, concat_axis=1, tiled=True)]
    dot_general x22 -> x8, matrix products: 84.7 us -> 33.7 us  [contract(): lax.dot_general(left, right, (((left_dim,), (right_dim,)), ((), ())), pre...]
    all_gather x1 -> x0, blocking collectives: 51 us -> none  [gather_rows(): return lax.all_gather(low(share), ALL, axis=0, tiled=True)]
    concatenate x7 -> x1, local copies, waits for them, and re-layouts: 38.6 us -> 0.01 us  [own_biases(): lines = jnp.concatenate(parts).reshape(-1, 128)]
  transfers between devices with their start and end apart: 18 -> 8, of which waited for: 11 -> 6; matrix products, arithmetic and copies ran while one was open for 18% -> 10% of each run, Pallas kernels for 0% -> 0%
where the time goes in v2:
time: 985 us; the launch traced here: 975 us
  waiting for transfers between devices  368 us (37%)
  Pallas kernels  163 us (17%)
  blocking collectives  123 us (12%)
  matrix products  120 us (12%)
  local copies, waits for them, and re-layouts  96.7 us (10%)
  other arithmetic  64.9 us (7%)
  starting transfers between devices  23.7 us (2%)
  between operations  15.8 us (2%)
    reduce_scatter x4, waiting for transfers between devices, scatter_rows(): return lax.psum_scatter(whole, ALL, scatter_dimension=0, tiled=True)  340 us
    pallas_call x1, Pallas kernels, run_forward(): pl.pallas_call(forward_kernel, out_shape=[shape(*out) for out in outs], i...  163 us
    all_gather x1, blocking collectives, frame_gradients(): every = lax.all_gather(grad_modulation, ALL, axis=0, tiled=True)  44.4 us
    all_gather x1, blocking collectives, frame_gradients(): lax.all_gather(silu_back(grad_silu)[0], ALL, axis=1, tiled=True)  40.6 us
    unnamed x6, other arithmetic  38.4 us
    unnamed x1, blocking collectives  37.6 us
    dot_general x8, matrix products, contract(): lax.dot_general(left, right, (((left_dim,), (right_dim,)), ((), ())), pre...  33.7 us
    dot_general x8, matrix products, one_block(): jnp.einsum('chqk,cqhd->ckhd', low(softmax_weights), grad_block, preferred...  25.9 us
  transfers between devices with their start and end apart: 8, of which 6 were waited for; matrix products, arithmetic and copies ran while one was open for 10% of the time, Pallas kernels for 0%

profile of v2, /device:TPU:0, one launch (start us, length us, event | category | flops | bytes accessed | tf_op | source)
XLA Modules:
  0.0 974.6 jit_solution(4288880176259980079)
XLA Ops:
  15.2 162.8 %block_forward.1 = (bf16[256,1024]{1,0:T(8,128)(2,1)}, bf16[8,4,4,2,32,1024]{5,4,3,2,1,0:T(8,128)(2,1)}, bf16[4,4,4,2,128,256]{5,4,3,2,1,0:T(8,128)(2,1)}, bf16[...) custom-call(bf16[256,1024]{1,0:T(8,128)(2,1)} %bitcast.273, ...), custom_call_target="tpu_custom_call" | custom-call | tf_op jit(solution)/shard_map/block_forward/pallas_call | solution.py:891
  178.0 8.5 slice.91
  189.8 11.8 %copy.118 = bf16[4,4096,256]{1,2,0:T(8,128)(2,1)} copy(bf16[4,4096,256]{2,1,0:T(8,128)(2,1)} %bitcast.274) | data formatting | bytes 16777216 | tf_op jit(solution)/shard_map/reshape | solution.py:977
  202.0 11.4 %copy.119 = bf16[4,1024,1024]{1,2,0:T(8,128)(2,1)} copy(bf16[4,1024,1024]{2,1,0:T(8,128)(2,1)} %bitcast.271) | data formatting | bytes 16777216 | tf_op jit(solution)/shard_map/slice | solution.py:991
  213.4 6.5 convert_reduce_fusion
  231.5 11.4 %all-to-all-start = ((bf16[8,2,16384]{2,1,0:T(2,128)(2,1)}), bf16[8,2,16384]{2,1,0:T(2,128)(2,1)S(1)}, u32[]{:S(2)}, u32[]{:S(2)}) async-start(bf16[8,2,16384]{2,1,0:T(2,128)(2,1)} %reshape.669), calls=%async_computation | async-start | bytes 1048576 | tf_op jit(solution)/shard_map/all_to_all | solution.py:127
  246.1 12.1 %all-to-all-done = bf16[8,2,16384]{2,1,0:T(2,128)(2,1)S(1)} async-done(((bf16[8,2,16384]{2,1,0:T(2,128)(2,1)}), bf16[8,2,16384]{2,1,0:T(2,128)(2,1)S(1)}, u32[]{:S(2)}, u32[]{:S(2)}) %all-to-all-start) | async-done | bytes 524320 | tf_op jit(solution)/shard_map/all_to_all | solution.py:127
  262.9 98.8 %while.17 = (s32[]{:T(128)}, f32[1,2048,2,64]{1,3,2,0:T(8,128)}, f32[1,2048,2,64]{1,3,2,0:T(8,128)}, bf16[8,1,256,2,64]{2,4,3,1,0:T(8,128)(2,1)}, bf16[8,1,256,2...) while((s32[]{:T(128)}, f32[1,2048,2,64]{1,3,2,0:T(8,128)}, ...), condition=%wide.region_6.7_spmd.clone, body=%wide.region_5.6_spmd.clone.sunk | while | flops 680544256 | bytes 67004748 | solution.py:190
  364.7 11.5 %reduce.6 = bf16[2048,128]{1,0:T(8,128)(2,1)S(1)} reduce(bf16[2048,1,128]{2,1,0:T(2,128)(2,1)S(1)} %bitcast.286, bf16[]{:T(256)} %broadcast.491), dimensions={1}, to_apply=%bitcast.213.reduce_sub_computation | reduce | bytes 1048578
  381.7 11.5 %reduce.5 = bf16[2048,128]{1,0:T(8,128)(2,1)S(1)} reduce(bf16[2048,1,128]{2,1,0:T(2,128)(2,1)S(1)} %bitcast.287, bf16[]{:T(256)} %broadcast.491), dimensions={1}, to_apply=%bitcast.211.reduce_sub_computation | reduce | bytes 1048578
  404.9 11.5 %reduce.4 = bf16[2048,128]{1,0:T(8,128)(2,1)S(1)} reduce(bf16[2048,1,128]{2,1,0:T(2,128)(2,1)S(1)} %bitcast.285, bf16[]{:T(256)} %broadcast.491), dimensions={1}, to_apply=%bitcast.209.reduce_sub_computation | reduce | bytes 1048578
  417.3 5.0 all-to-all-start.3
  426.3 14.0 %all-to-all-done.3 = bf16[8,2,16384]{2,1,0:T(2,128)(2,1)} async-done(((bf16[8,2,16384]{2,1,0:T(2,128)(2,1)}), bf16[8,2,16384]{2,1,0:T(2,128)(2,1)}, u32[]{:S(2)}, u32[]{:S(2)}) %all-to-all-start.3) | async-done | bytes 524320 | tf_op jit(solution)/shard_map/all_to_all | solution.py:131
  454.5 5.6 convolution_convert_fusion.1
  461.9 5.6 convolution_convert_fusion
  467.5 6.7 slice.112
  474.3 9.0 copy.138
  484.0 4.9 fusion.36
  491.1 37.6 %all-reduce.5 = (f32[3072]{0:T(1024)S(1)}, f32[1024]{0:T(1024)S(1)}, f32[4096]{0:T(1024)S(1)}, f32[1024]{0:T(1024)S(1)}) all-reduce(f32[3072]{0:T(1024)S(1)} %convert_reduce_fusion.1, f32[1024]{0:T(1024)S(1)} %get-tuple-element.332, f32[4096]{0:T(1024)S(1)} %get-tuple-element.367, ...), channel_id=3, replica_groups=mesh['dp'=4,'seq'=8] {'dp','seq'}, use_global_device_ids=true, to_apply=%region_19.20.clone | all-reduce | flops 9216 | bytes 73728
  531.1 44.4 %all-gather = bf16[32,1,6144]{2,1,0:T(2,128)(2,1)S(1)} all-gather(bf16[1,1,6144]{2,1,0:T(2,128)(2,1)S(1)} %bitcast.316), channel_id=1, replica_groups=mesh['dp'=4,'seq'=8] {'dp','seq'}, dimensions={0}, use_global_device_ids=true | all-gather | bytes 405504 | tf_op jit(solution)/shard_map/all_gather | solution.py:107
  576.6 40.6 %all_gather.7 = f32[32,1024]{0,1:T(8,128)S(1)} all-gather(f32[32,32]{0,1:T(8,128)S(1)} %fusion.59), channel_id=1, replica_groups=mesh['dp'=4,'seq'=8] {'dp','seq'}, dimensions={1}, use_global_device_ids=true | all-gather | bytes 135168 | tf_op jit(solution)/shard_map/all_gather | solution.py:119
  622.0 37.6 %reduce-scatter.5.cloned.1.call-done = bf16[32,3072]{1,0:T(8,128)(2,1)} async-done(((bf16[1024,3072]{1,0:T(8,128)(2,1)}), bf16[32,3072]{1,0:T(8,128)(2,1)}) %reduce-scatter.5.cloned.1.call-update) | async-done | bytes 196624 | tf_op jit(solution)/shard_map/reduce_scatter | solution.py:88
  661.3 152.3 %reduce-scatter.9.cloned.1.call-done = bf16[32,4096]{1,0:T(8,128)(2,1)} async-done(((bf16[1024,4096]{1,0:T(8,128)(2,1)}), bf16[32,4096]{1,0:T(8,128)(2,1)}) %reduce-scatter.9.cloned.1.call-update) | async-done | bytes 262160 | tf_op jit(solution)/shard_map/reduce_scatter | solution.py:88
  815.4 149.6 %reduce-scatter.11.cloned.1.call-done = bf16[128,1024]{1,0:T(8,128)(2,1)} async-done(((bf16[4096,1024]{1,0:T(8,128)(2,1)}), bf16[128,1024]{1,0:T(8,128)(2,1)}) %reduce-scatter.11.cloned.1.call-update) | async-done | bytes 262160 | tf_op jit(solution)/shard_map/reduce_scatter | solution.py:88
  (382 shorter events, 186.2 us)
Async XLA Ops:
  189.7 11.8 %copy-start.5 = (f32[256,1024]{1,0:T(8,128)S(1)}, f32[256,1024]{1,0:T(8,128)}, u32[]{:S(2)}) copy-start(f32[256,1024]{1,0:T(8,128)} %get-tuple-element.177) | copy-start | bytes 3145732
  202.0 11.4 %copy-start.8 = (bf16[1,256,1024]{2,1,0:T(8,128)(2,1)S(1)}, bf16[1,256,1024]{2,1,0:T(8,128)(2,1)}, u32[]{:S(2)}) copy-start(bf16[1,256,1024]{2,1,0:T(8,128)(2,1)} %param.29) | copy-start | bytes 1572868
  213.4 6.5 copy-start.7
  224.2 6.3 copy-start.22
  225.3 17.6 %copy-start.29 = (bf16[8,256,128]{2,1,0:T(8,128)(2,1)S(1)}, bf16[8,256,128]{2,1,0:T(8,128)(2,1)}, u32[]{:S(2)}) copy-start(bf16[8,256,128]{2,1,0:T(8,128)(2,1)} %get-tuple-element.182) | copy-start | bytes 1572868
  231.5 13.0 %copy-start.33 = (bf16[8,256,128]{2,1,0:T(8,128)(2,1)S(1)}, bf16[8,256,128]{2,1,0:T(8,128)(2,1)}, u32[]{:S(2)}) copy-start(bf16[8,256,128]{2,1,0:T(8,128)(2,1)} %get-tuple-element.179) | copy-start | bytes 1572868
  231.5 26.7 %all-to-all-start = ((bf16[8,2,16384]{2,1,0:T(2,128)(2,1)}), bf16[8,2,16384]{2,1,0:T(2,128)(2,1)S(1)}, u32[]{:S(2)}, u32[]{:S(2)}) async-start(bf16[8,2,16384]{2,1,0:T(2,128)(2,1)} %reshape.669), calls=%async_computation | async-start | bytes 1048576 | tf_op jit(solution)/shard_map/all_to_all | solution.py:127
  364.0 16.8 %copy-start.2 = (f32[1,2048,2,64]{1,3,2,0:T(8,128)S(1)}, f32[1,2048,2,64]{1,3,2,0:T(8,128)}, u32[]{:S(2)}) copy-start(f32[1,2048,2,64]{1,3,2,0:T(8,128)} %get-tuple-element.184) | copy-start | bytes 3145732
  377.1 18.9 %all-to-all-start.1 = ((bf16[8,2,16384]{2,1,0:T(2,128)(2,1)}), bf16[8,2,16384]{2,1,0:T(2,128)(2,1)S(1)}, u32[]{:S(2)}, u32[]{:S(2)}) async-start(bf16[8,2,16384]{2,1,0:T(2,128)(2,1)} %reshape.675), calls=%async_computation.1 | async-start | bytes 1048576 | tf_op jit(solution)/shard_map/all_to_all | solution.py:131
  380.8 18.8 %copy-start.23 = (bf16[256,1024]{1,0:T(8,128)(2,1)S(1)}, bf16[256,1024]{1,0:T(8,128)(2,1)}, u32[]{:S(2)}) copy-start(bf16[256,1024]{1,0:T(8,128)(2,1)} %copy-done.22) | copy-start | bytes 1572868
  396.1 21.2 %all-to-all-start.2 = ((bf16[8,2,16384]{2,1,0:T(2,128)(2,1)}), bf16[8,2,16384]{2,1,0:T(2,128)(2,1)S(1)}, u32[]{:S(2)}, u32[]{:S(2)}) async-start(bf16[8,2,16384]{2,1,0:T(2,128)(2,1)} %reshape.673), calls=%async_computation.2 | async-start | bytes 1048576 | tf_op jit(solution)/shard_map/all_to_all | solution.py:131
  399.6 220.9 %reduce-scatter.7.cloned.1.call-start = ((), (), s32[]{:S(2)}) async-start(), calls=%async_computation.9 | async-start | bytes 2162688 | tf_op jit(solution)/shard_map/reduce_scatter | solution.py:88
  417.3 22.9 %all-to-all-start.3 = ((bf16[8,2,16384]{2,1,0:T(2,128)(2,1)}), bf16[8,2,16384]{2,1,0:T(2,128)(2,1)}, u32[]{:S(2)}, u32[]{:S(2)}) async-start(bf16[8,2,16384]{2,1,0:T(2,128)(2,1)} %reshape.671), calls=%async_computation.3 | async-start | bytes 1048576 | tf_op jit(solution)/shard_map/all_to_all | solution.py:131
  422.3 237.3 %reduce-scatter.5.cloned.1.call-start = ((), (), s32[]{:S(2)}) async-start(), calls=%async_computation.8 | async-start | bytes 6488064 | tf_op jit(solution)/shard_map/reduce_scatter | solution.py:88
  452.8 360.8 %reduce-scatter.9.cloned.1.call-start = ((), (), s32[]{:S(2)}) async-start(), calls=%async_computation.10 | async-start | bytes 8650752 | tf_op jit(solution)/shard_map/reduce_scatter | solution.py:88
  460.1 504.9 %reduce-scatter.11.cloned.1.call-start = ((), (), s32[]{:S(2)}) async-start(), calls=%async_computation.11 | async-start | bytes 8650752 | tf_op jit(solution)/shard_map/reduce_scatter | solution.py:88
  474.2 9.1 copy-start.6
  474.2 9.2 copy-start.17
  474.2 9.2 copy-start.25
  474.2 9.2 copy-start.27
  488.9 42.1 %copy-start.38 = (f32[1,1024]{1,0:T(1,128)S(1)}, f32[1,1024]{1,0:T(1,128)}, u32[]{:S(2)}) copy-start(f32[1,1024]{1,0:T(1,128)} %get-tuple-element.188) | copy-start | bytes 12292
  489.5 86.7 %copy-start.13 = (f32[32,6144]{1,0:T(8,128)S(1)}, f32[32,6144]{1,0:T(8,128)}, u32[]{:S(2)}) copy-start(f32[32,6144]{1,0:T(8,128)} %w_ada_ref.1) | copy-start | bytes 2359300
  489.5 86.7 %copy-start.35 = (f32[32,128]{1,0:T(8,128)S(1)}, f32[32,128]{1,0:T(8,128)}, u32[]{:S(2)}) copy-start(f32[32,128]{1,0:T(8,128)} %get-tuple-element.189) | copy-start | bytes 49156
  575.5 391.3 %copy-start.30 = (bf16[256,1024]{1,0:T(8,128)(2,1)S(1)}, bf16[256,1024]{1,0:T(8,128)(2,1)}, u32[]{:S(2)}) copy-start(bf16[256,1024]{1,0:T(8,128)(2,1)} %get-tuple-element.172) | copy-start | bytes 1572868
  (66 other events, 186.2 us)
Sparse Core Ops, SparseCore 0:
  402.9 138.5 reduce-scatter.6
  548.1 111.4 reduce-scatter.4
  661.9 151.6 reduce-scatter.8
  815.8 149.1 reduce-scatter.10
